TPU v7x, 32 devices: a whole 2x2x4 slice. The times are simulated.
32 devices in a mesh: row: 8 (over z, x), col: 4 (over y, core).
Axes of the slice: x: 2, y: 2, z: 4, core: 2. Of those that a mesh axis runs over, the one named last changes fastest.
Arguments:
- arriving: float32 [16384, 256], P(('row', 'col')), may hold values from -0.6 to 0.6
- expiring: float32 [16384, 256], P(('row', 'col')), may hold values from -0.6 to 0.6
- taps: float32 [9], replicated, may hold values from -1.4 to 1.4
- covariance: float32 [16384, 16384], P('row', 'col'), may hold values from -1 to 6, as said below
- vectors: float32 [16384, 256], P(('row', 'col')), may hold values from -6 to 6
Outputs:
- updated: float32 [16384, 16384], P('row', 'col')
- basis: float32 [16384, 256], P(('row', 'col'))
Inputs may be any that keep to these rules, and one draw needn't show every extreme that they name: `covariance`: symmetric.
All inputs are finite; a program needn't handle non-finite values.
Results may differ from a plain program's by a relative error of at most 0.0013.
Values may be sent and summed in bfloat16 or wider, within the bound.
No kernel may reach another device: no remote copies, remote signals or barrier semaphores. Data moves between devices by JAX's collectives and lax.ppermute only.
A program may use at most 192 MiB of HBM per device.

v0:
```python
import jax
import jax.numpy as jnp
from jax import lax
from jax.sharding import PartitionSpec as P

CH = 16384
TAPS = 9
HALF = 4


def padded_2(cells, sides, width):
    for axis, dim in sides:
        count = lax.axis_size(axis)
        ends = count - 1
        head = lax.slice_in_dim(cells, 0, width, axis=dim)
        tail = lax.slice_in_dim(cells, cells.shape[dim] - width, cells.shape[dim], axis=dim)
        cells = jnp.concatenate(
            [
                lax.ppermute(tail, axis, [(i, (i + 1) % count) for i in range(ends)]),
                cells,
                lax.ppermute(head, axis, [((i + 1) % count, i) for i in range(ends)]),
            ],
            axis=dim,
        )
    return cells


def shards(arriving, expiring, taps, covariance, vectors):
    stripe = arriving.shape[0]
    samples = arriving.shape[1]
    raw = jnp.concatenate([arriving, expiring], 1)
    padded = padded_2(raw, ((("row", "col"), 0),), HALF)
    total = jnp.zeros(raw.shape, jnp.float32)
    for tap in range(TAPS):
        total = total + taps[tap] * padded[tap : tap + stripe]
    filtered = total.astype(jnp.bfloat16)
    row_data = lax.all_gather(filtered, "col", axis=0, tiled=True)
    col_index = lax.axis_index("col")
    width = covariance.shape[1]
    everything = lax.all_gather(filtered, ("row", "col"), axis=0, tiled=True)
    col_data = lax.dynamic_slice_in_dim(everything, col_index * width, width, 0)
    signed = jnp.concatenate([col_data[:, :samples], -col_data[:, samples:]], 1)
    change = lax.dot_general(
        row_data, signed, (((1,), (1,)), ((), ())), preferred_element_type=jnp.float32
    )
    updated = covariance + change / samples
    row_vectors = lax.all_gather(vectors, "col", axis=0, tiled=True)
    block = updated
    piece = lax.psum_scatter(
        lax.dot_general(
            block,
            row_vectors,
            (((0,), (0,)), ((), ())),
            precision=lax.Precision.HIGHEST,
            preferred_element_type=jnp.float32,
        ),
        "row",
        scatter_dimension=0,
        tiled=True,
    )
    first_column = lax.all_gather(piece, "row", axis=0, tiled=True)
    block = updated
    second = lax.psum_scatter(
        jnp.dot(
            block, first_column, precision=lax.Precision.HIGHEST, preferred_element_type=jnp.float32
        ),
        "col",
        scatter_dimension=0,
        tiled=True,
    )
    local_gram = jnp.dot(
        second.T, second, precision=lax.Precision.HIGHEST, preferred_element_type=jnp.float32
    )
    gram = lax.psum(local_gram, ("row", "col")) / CH
    factor = jnp.linalg.cholesky(gram)
    basis = jax.scipy.linalg.solve_triangular(factor, second.T, lower=True).T
    return (updated, basis)


def solution(mesh):
    in_specs = (
        P(("row", "col"), None),
        P(("row", "col"), None),
        P(),
        P("row", "col"),
        P(("row", "col"), None),
    )
    out_specs = (P("row", "col"), P(("row", "col"), None))
    return jax.shard_map(shards, mesh=mesh, in_specs=in_specs, out_specs=out_specs, check_vma=False)
```

profile of v0, /device:TPU:0, one launch (start us, length us, event | category | flops | bytes accessed | tf_op | source)
XLA Modules:
  0.0 680.2 jit_solution(693701402077632646)
XLA Ops:
  7.2 0.0 all-gather.7.cloned.1.call-start
  7.2 1.1 constant_dynamic-update-slice_fusion.1
  8.3 1.1 constant_dynamic-update-slice_fusion
  9.5 2.4 collective-permute-start
  11.8 1.3 collective-permute-start.1
  13.1 1.7 fusion.37
  14.8 2.2 collective-permute-done.1
  17.0 7.7 %fusion.7 = bf16[512,512]{1,0:T(8,128)(2,1)} fusion(f32[4,512]{1,0:T(4,128)S(1)} %collective-permute-done.1, f32[4,512]{1,0:T(4,128)S(1)} %collective-permute-done, f32[512,512]{1,0:T(8,128)S(1)} %constant_dynamic-update-slice_fusion, f32[]{:T(128)} %bitcast.8, f32[]{:T(128)} %bitcast.7, f32[]{:T(128)} %bitcast.6, f32[]{:T(128)} %bitcast.5, f32[]{:T(128)} %bitcast.4, ...), kind=kLoop, calls=%fused_computation.19 | loop fusion | flops 6815744 | bytes 1589284 | tf_op jit(solution)/shard_map/convert_element_type | solution.py:36
  24.7 0.0 all-gather.5.cloned.1.call-start
  24.8 0.7 all-gather.5.cloned.1.call-update
  25.5 0.0 all-gather.9.cloned.1.call-start
  25.5 0.7 all-gather.9.cloned.1.call-update
  26.2 0.0 reduce-scatter.3.cloned.1.call-start
  26.3 117.5 %all-gather.7.cloned.1.call-done = bf16[16384,512]{1,0:T(8,128)(2,1)} async-done(((bf16[512,512]{1,0:T(8,128)(2,1)}), bf16[16384,512]{1,0:T(8,128)(2,1)}) %all-gather.7.cloned.1.call-update) | async-done | bytes 16777232 | tf_op jit(solution)/shard_map/all_gather | solution.py:40
  143.8 4.0 constant_dynamic-slice_fusion.1
  147.8 18.9 %all-gather.5.cloned.1.call-done = bf16[2048,512]{1,0:T(8,128)(2,1)} async-done(((bf16[512,512]{1,0:T(8,128)(2,1)}), bf16[2048,512]{1,0:T(8,128)(2,1)}) %all-gather.5.cloned.1.call-update) | async-done | bytes 2097168 | tf_op jit(solution)/shard_map/all_gather | solution.py:37
  166.7 27.9 %multiply_add_fusion = f32[2048,4096]{1,0:T(8,128)} fusion(f32[2048,4096]{1,0:T(8,128)} %param.8, bf16[2048,512]{1,0:T(8,128)(2,1)} %all-gather.5.cloned.1.call-done, bf16[4096,256]{1,0:T(8,128)(2,1)} %get-tuple-element.23, bf16[4096,256]{1,0:T(8,128)(2,1)S(1)} %get-tuple-element.22), kind=kOutput, calls=%fused_computation.2 | convolution fusion | flops 8615100416 | bytes 73400320 | tf_op jit(solution)/shard_map/dot_general | solution.py:43
  194.6 58.0 %fusion.38 = f32[4096,256]{1,0:T(8,128)} fusion(f32[2048,4096]{1,0:T(8,128)} %multiply_add_fusion, f32[2048,256]{1,0:T(8,128)} %all-gather.9.cloned.1.call-done), kind=kOutput, calls=%fused_computation.74 | convolution fusion | flops 25769803776 | bytes 39845888 | tf_op jit(solution)/shard_map/dot_general | solution.py:50
  252.6 0.0 reduce-scatter.3.cloned.1.call-update
  252.6 0.0 all-gather.11.cloned.1.call-start
  252.7 88.2 %reduce-scatter.3.cloned.1.call-done = f32[512,256]{1,0:T(8,128)} async-done(((f32[4096,256]{1,0:T(8,128)}), f32[512,256]{1,0:T(8,128)}) %reduce-scatter.3.cloned.1.call-update) | async-done | bytes 524304 | tf_op jit(solution)/shard_map/reduce_scatter | solution.py:49
  340.9 0.0 reduce-scatter.5.cloned.1.call-start
  340.9 75.3 %all-gather.11.cloned.1.call-done = f32[4096,256]{1,0:T(8,128)} async-done(((f32[512,256]{1,0:T(8,128)}), f32[4096,256]{1,0:T(8,128)}) %all-gather.11.cloned.1.call-update) | async-done | bytes 4194320 | tf_op jit(solution)/shard_map/all_gather | solution.py:61
  416.2 31.5 %fusion.39 = f32[2048,256]{1,0:T(8,128)} fusion(f32[2048,4096]{1,0:T(8,128)} %multiply_add_fusion, f32[4096,256]{1,0:T(8,128)} %all-gather.11.cloned.1.call-done), kind=kOutput, calls=%fused_computation.75 | convolution fusion | flops 25769803776 | bytes 39845888 | tf_op jit(solution)/shard_map/dot_general | solution.py:64
  447.7 0.0 all-reduce.3.cloned.1.call-start
  447.8 29.8 %reduce-scatter.5.cloned.1.call-done = f32[512,256]{1,0:T(8,128)} async-done(((f32[2048,256]{1,0:T(8,128)}), f32[512,256]{1,0:T(8,128)}) %reduce-scatter.5.cloned.1.call-update) | async-done | bytes 524304 | tf_op jit(solution)/shard_map/reduce_scatter | solution.py:63
  477.6 3.0 fusion.40
  480.6 128.0 %all-reduce.3.cloned.1.call-done = f32[256,256]{0,1:T(8,128)} async-done(((f32[256,256]{0,1:T(8,128)}), f32[256,256]{0,1:T(8,128)}) %all-reduce.3.cloned.1.call-update) | async-done | bytes 262160 | tf_op jit(solution)/shard_map/psum | solution.py:74
  608.6 1.0 broadcast_multiply_fusion
  609.6 0.1 copy.8
  609.7 1.0 fusion.28
  610.7 11.7 %cholesky.50 = f32[128,128]{1,0:T(8,128)S(1)} custom-call(f32[128,128]{1,0:T(8,128)S(1)} %cholesky.118), custom_call_target="Cholesky" | custom-call | tf_op jit(solution)/shard_map/jit(cholesky)/cholesky | solution.py:75
  622.5 9.8 %custom-call.15 = f32[1,128,128]{1,2,0:T(8,128)S(1)} custom-call(f32[1,128,128]{2,1,0:T(8,128)S(1)} %get-tuple-element.29), custom_call_target="InvertDiagBlocksLowerTriangular" | custom-call | tf_op jit(solution)/shard_map/jit(cholesky)/cholesky | solution.py:75
  632.3 0.2 constant_dynamic-update-slice_fusion.3
  632.5 0.3 convolution_subtract_fusion.1
  632.8 11.7 %cholesky.105 = f32[128,128]{1,0:T(8,128)S(1)} custom-call(f32[128,128]{1,0:T(8,128)S(1)} %convolution_subtract_fusion.1), custom_call_target="Cholesky" | custom-call | tf_op jit(solution)/shard_map/jit(cholesky)/cholesky | solution.py:75
  644.5 0.7 compare_reduce_fusion
  646.5 0.1 triangular_solve.57
  646.6 4.2 while.1
  646.8 0.6 fusion.53
  647.4 1.4 bitcast_dynamic-update-slice_fusion.2
  648.8 0.6 fusion.53
  649.4 1.4 bitcast_dynamic-update-slice_fusion.2
  650.8 19.7 %custom-call.16 = f32[2,128,128]{1,2,0:T(8,128)S(1)} custom-call(f32[2,128,128]{2,1,0:T(8,128)S(1)} %get-tuple-element.9), custom_call_target="InvertDiagBlocksLowerTriangular" | custom-call | tf_op jit(solution)/shard_map/jit(_solve_triangular)/triangular_solve | solution.py:76
  670.4 0.4 fusion.26
  670.9 0.6 convolution_subtract_fusion
  671.5 0.4 fusion.30
  671.9 1.0 copy.9
  (19 shorter events, 0.3 us)
Async XLA Ops:
  7.2 136.6 %all-gather.7.cloned.1.call-start = ((), (), s32[]{:S(2)}) async-start(), calls=%async_computation.3 | async-start | bytes 17301504 | tf_op jit(solution)/shard_map/all_gather | solution.py:40
  9.5 5.3 collective-permute-start
  11.8 5.2 collective-permute-start.1
  24.7 142.0 %all-gather.5.cloned.1.call-start = ((), (), s32[]{:S(2)}) async-start(), calls=%async_computation.2 | async-start | bytes 2621440 | tf_op jit(solution)/shard_map/all_gather | solution.py:37
  25.5 169.1 %all-gather.9.cloned.1.call-start = ((), (), s32[]{:S(2)}) async-start(), calls=%async_computation.4 | async-start | bytes 2621440 | tf_op jit(solution)/shard_map/all_gather | solution.py:47
  26.2 314.6 %reduce-scatter.3.cloned.1.call-start = ((), (), s32[]{:S(2)}) async-start(), calls=%async_computation.5 | async-start | bytes 4718592 | tf_op jit(solution)/shard_map/reduce_scatter | solution.py:49
  252.6 163.6 %all-gather.11.cloned.1.call-start = ((), (), s32[]{:S(2)}) async-start(), calls=%async_computation.6 | async-start | bytes 4718592 | tf_op jit(solution)/shard_map/all_gather | solution.py:61
  340.9 136.7 %reduce-scatter.5.cloned.1.call-start = ((), (), s32[]{:S(2)}) async-start(), calls=%async_computation.7 | async-start | bytes 2621440 | tf_op jit(solution)/shard_map/reduce_scatter | solution.py:63
  447.7 160.9 %all-reduce.3.cloned.1.call-start = ((), (), s32[]{:S(2)}) async-start(), calls=%async_computation.8 | async-start | bytes 524288 | tf_op jit(solution)/shard_map/psum | solution.py:74
  477.6 192.9 %copy-start = (f32[512,256]{1,0:T(8,128)S(1)}, f32[512,256]{1,0:T(8,128)}, u32[]{:S(2)}) copy-start(f32[512,256]{1,0:T(8,128)} %reduce-scatter.5.cloned.1.call-done) | copy-start | bytes 1572868
Sparse Core Ops, SparseCore 0:
  24.8 118.9 all-gather.6
  145.9 20.7 all-gather.4
  168.3 22.5 all-gather.8
  252.7 88.0 reduce-scatter.2
  343.0 73.1 all-gather.10
  447.8 29.6 reduce-scatter.4
  483.6 124.9 all-reduce.2
where the time goes:
time: 689 us; the launch traced here: 680 us
  waiting for transfers between devices  461 us (67%)
  matrix products  122 us (18%)
  other arithmetic  67.3 us (10%)
  between operations  16 us (2%)
  local copies, waits for them, and re-layouts  9.01 us (1%)
    psum x1, waiting for transfers between devices, shards(): gram = lax.psum(local_gram, ('row', 'col')) / CH  128 us
    all_gather x1, waiting for transfers between devices, shards(): everything = lax.all_gather(filtered, ('row', 'col'), axis=0, tiled=True)  118 us
    reduce_scatter x1, waiting for transfers between devices, shards(): lax.psum_scatter(lax.dot_general(block, row_vectors, (((0,), (0,)), ((),...  88.2 us
    all_gather x1, waiting for transfers between devices, shards(): first_column = lax.all_gather(piece, 'row', axis=0, tiled=True)  75.3 us
    dot_general x1, matrix products, shards(): lax.dot_general(block, row_vectors, (((0,), (0,)), ((), ())), precision=l...  58 us
    another operation x6, other arithmetic, shards(): factor = jnp.linalg.cholesky(gram)  34 us
    dot_general x1, matrix products, shards(): jnp.dot(block, first_column, precision=lax.Precision.HIGHEST, preferred_e...  31.5 us
    reduce_scatter x1, waiting for transfers between devices, shards(): lax.psum_scatter(jnp.dot(block, first_column, precision=lax.Precision.HIG...  29.8 us
  transfers between devices with their start and end apart: 9, of which 7 were waited for; matrix products, arithmetic and copies ran while one was open for 5% of the time, Pallas kernels for 0%

commit v1 on v0

v1 whole, which is shorter than its diff:
```python
import functools
import math

import jax
import jax.numpy as jnp
from jax import lax
from jax.experimental import pallas as pl
from jax.experimental.pallas import tpu as pltpu
from jax.sharding import PartitionSpec as P

HIGHEST = lax.Precision.HIGHEST
F32, F16, BF16 = jnp.float32, jnp.float16, jnp.bfloat16
VMEM_LIMIT = 40 * 1024 * 1024


def swap(cells, axis, mask):
    return lax.ppermute(cells, axis, [(i, i ^ mask) for i in range(lax.axis_size(axis))])


def bits_of(axis):
    return [1 << b for b in range(lax.axis_size(axis).bit_length() - 1)]


def is_set(axis, mask):
    return (lax.axis_index(axis) & mask) != 0


def pick(upper, first, second):
    return jnp.where(upper, second, first)


def room(bound):
    return 2.0 ** (15 - math.ceil(math.log2(bound)))


def power_of_two_for(value):
    exponent = jnp.floor(jnp.log2(jnp.maximum(value, 1e-30)))
    return lax.reduce_precision(jnp.exp2(-exponent - 1.0), 8, 3)


def after(values, earlier):
    corner = lax.slice(earlier, (0,) * earlier.ndim, (1,) * earlier.ndim)
    entry = corner.reshape(()).astype(F32)
    return values + jnp.where(jnp.isnan(entry), 1, 0).astype(values.dtype)


def gather_pairs(cells, axis):
    blocks = {0: cells}
    for mask in reversed(bits_of(axis)):
        for known in list(blocks):
            blocks[known | mask] = swap(blocks[known], axis, mask)
    return [blocks[mask] for mask in range(lax.axis_size(axis))]


def scatter_sum(cells):
    for mask in bits_of("col"):
        half = cells.shape[0] // 2
        upper = is_set("col", mask)
        low, high = cells[:half], cells[half:]
        cells = pick(upper, low, high) + swap(pick(upper, high, low), "col", mask)
    return cells


def sum_over_row(cells):
    for mask in bits_of("row"):
        cells = cells + swap(cells, "row", mask)
    return cells


def gather_parts(cells):
    for mask in reversed(bits_of("col")):
        other = swap(cells, "col", mask)
        upper = is_set("col", mask)
        cells = jnp.concatenate([pick(upper, cells, other), pick(upper, other, cells)], 0)
    return cells


def largest_everywhere(value, planes):
    value = jnp.full((8, 128), value)
    for other in [swap(value, "row", 2 * j) for j in range(1, planes)]:
        value = jnp.maximum(value, other)
    value = jnp.maximum(value, swap(value, "row", 1))
    for mask in bits_of("col"):
        value = jnp.maximum(value, swap(value, "col", mask))
    return value


def halves(values):
    high = lax.reduce_precision(values, 8, 7)
    return high.astype(BF16), (values - high).astype(BF16)


def split(values):
    high = values.astype(BF16)
    return high, (values - high.astype(F32)).astype(BF16)


def first_kernel(blocks, place, extra, *refs):
    vectors, tiles = refs[:blocks], refs[blocks : 2 * blocks]
    send, keep = refs[2 * blocks :]
    count = send.shape[0]
    total = None
    for part, tile in zip(vectors, tiles):
        high, low = split(tile[...])
        both = jnp.dot(part[...], high, preferred_element_type=F32)
        rest = jnp.dot(part[:count], low, preferred_element_type=F32)
        term = both[:count] + both[count:] + rest
        total = term if total is None else total + term

    @pl.when(pl.program_id(0) == 0)
    def _():
        send[:, : total.shape[1]] = total
        send[:, total.shape[1] :] = extra[...]

    @pl.when(pl.program_id(0) == 1)
    def _():
        keep[:, : total.shape[1]] = total
        keep[:, total.shape[1] :] = extra[...]


def first_part(vectors, tile, extra, z, x, column, stripe):
    rows = tile.shape[0]
    blocks = len(vectors)
    count = vectors[0].shape[0] // 2
    depth = rows // blocks
    width = extra.shape[1]
    if stripe % 128:
        return first_part_plain(vectors, tile, extra, z, x, column, stripe)
    place = jnp.stack(
        [z * 2 + (1 - x), z * 2 + x] + [column ^ i for i in range(blocks)]
    ).astype(jnp.int32)

    def rows_of(member):
        return lambda i, p: (p[2 + member], p[i])

    shape = (count, stripe + width)
    return pl.pallas_call(
        functools.partial(first_kernel, blocks),
        grid_spec=pltpu.PrefetchScalarGridSpec(
            num_scalar_prefetch=1,
            grid=(2,),
            in_specs=[pl.BlockSpec((count, width), lambda i, p: (0, 0))]
            + [pl.BlockSpec((2 * count, depth), lambda i, p: (0, 0))] * blocks
            + [pl.BlockSpec((depth, stripe), rows_of(i)) for i in range(blocks)],
            out_specs=[pl.BlockSpec(shape, lambda i, p: (0, 0))] * 2,
        ),
        out_shape=[jax.ShapeDtypeStruct(shape, F32)] * 2,
        compiler_params=pltpu.CompilerParams(vmem_limit_bytes=VMEM_LIMIT),
        cost_estimate=pl.CostEstimate(
            flops=12 * count * rows * stripe, bytes_accessed=8 * rows * stripe, transcendentals=0
        ),
        name="first_part",
    )(place, extra, *vectors, *([tile] * blocks))


def first_part_plain(vectors, tile, extra, z, x, column, stripe):
    count = vectors[0].shape[0] // 2
    depth = tile.shape[0] // len(vectors)
    results = []
    for other in (1 - x, x):
        total = 0.0
        for i, part in enumerate(vectors):
            start = ((column ^ i) * depth, (z * 2 + other) * stripe)
            cells = lax.dynamic_slice(tile, start, (depth, stripe))
            values = part[:count].astype(F32) + part[count:].astype(F32)
            total = total + jnp.dot(values, cells, precision=HIGHEST)
        results.append(jnp.concatenate([total, extra], 1))
    return results


def second_part_plain(tile, entries, z, x, before):
    depth = entries[0].shape[0]
    total = 0.0 if before is None else before
    for i, other in enumerate((x, 1 - x)):
        start = (0, (z * 2 + other) * depth)
        cells = lax.dynamic_slice(tile, start, (tile.shape[0], depth))
        values = entries[2 * i].astype(F32) + entries[2 * i + 1].astype(F32)
        total = total + jnp.dot(cells, values, precision=HIGHEST)
    return total


def turn_kernel(cells, out):
    out[...] = cells[...].T


def turned(cells):
    return pl.pallas_call(
        turn_kernel,
        out_shape=jax.ShapeDtypeStruct(cells.shape[::-1], F32),
        compiler_params=pltpu.CompilerParams(vmem_limit_bytes=VMEM_LIMIT),
        name="turned",
    )(cells)


def second_kernel(started, place, *refs):
    tiles, entries = refs[:2], refs[2:6]
    out = refs[-1]
    total = refs[6][...] if started else None
    for tile, top, rest in zip(tiles, entries[::2], entries[1::2]):
        high, low = split(tile[...])
        term = (
            jnp.dot(high, top[...], preferred_element_type=F32)
            + jnp.dot(high, rest[...], preferred_element_type=F32)
            + jnp.dot(low, top[...], preferred_element_type=F32)
        )
        total = term if total is None else total + term
    out[...] = total


def second_part(tile, entries, z, x, before):
    rows = tile.shape[0]
    depth, count = entries[0].shape
    if depth % 128:
        return second_part_plain(tile, entries, z, x, before)
    block = min(rows, 512)
    specs = [
        pl.BlockSpec((block, depth), lambda i, p: (i, p[0])),
        pl.BlockSpec((block, depth), lambda i, p: (i, p[1])),
    ] + [pl.BlockSpec((depth, count), lambda i, p: (0, 0))] * 4
    operands = [tile, tile, *entries]
    total = pl.BlockSpec((block, count), lambda i, p: (i, 0))
    if before is not None:
        specs.append(total)
        operands.append(before)
    return pl.pallas_call(
        functools.partial(second_kernel, before is not None),
        grid_spec=pltpu.PrefetchScalarGridSpec(
            num_scalar_prefetch=1, grid=(rows // block,), in_specs=specs, out_specs=total
        ),
        out_shape=jax.ShapeDtypeStruct((rows, count), F32),
        compiler_params=pltpu.CompilerParams(vmem_limit_bytes=VMEM_LIMIT),
        cost_estimate=pl.CostEstimate(
            flops=12 * count * rows * depth, bytes_accessed=8 * rows * depth, transcendentals=0
        ),
        name="second_part",
    )(jnp.stack([z * 2 + x, z * 2 + (1 - x)]).astype(jnp.int32), *operands)


def update_kernel(scale, tile, rows, columns, *rest):
    change = lax.dot_general(
        rows[...], columns[...], (((1,), (1,)), ((), ())), preferred_element_type=F32
    )
    rest[-1][...] = tile[...] + change * scale


def update_part(tile, rows, columns, part, parts, before, scale):
    height, width = tile.shape
    depth = rows.shape[1]
    high = min(height // parts, 256)
    steps = height // parts // high
    specs = [
        pl.BlockSpec((high, width), lambda i: (part * steps + i, 0)),
        pl.BlockSpec((high, depth), lambda i: (part * steps + i, 0)),
        pl.BlockSpec((width, depth), lambda i: (0, 0)),
    ]
    operands = [tile, rows, columns]
    if before is not None:
        specs.append(pl.BlockSpec(memory_space=pl.ANY))
        operands.append(before)
    return pl.pallas_call(
        functools.partial(update_kernel, scale),
        grid=(steps,),
        in_specs=specs,
        out_specs=pl.BlockSpec((high, width), lambda i: (part * steps + i, 0)),
        out_shape=jax.ShapeDtypeStruct((height, width), F32),
        input_output_aliases={} if before is None else {3: 0},
        compiler_params=pltpu.CompilerParams(vmem_limit_bytes=VMEM_LIMIT),
        cost_estimate=pl.CostEstimate(
            flops=2 * height * width * depth // parts,
            bytes_accessed=8 * height * width // parts,
            transcendentals=0,
        ),
        name="update_part",
    )(*operands)


def filter_kernel(taps, arriving, expiring, above, below, out, work):
    stripe, samples = arriving.shape
    count = taps.shape[0]
    half = count // 2
    work[8 - half : 8, :] = above[...]
    work[8 : 8 + stripe, :samples] = arriving[...]
    work[8 : 8 + stripe, samples:] = expiring[...]
    work[8 + stripe : 8 + stripe + half, :] = below[...]
    step = 64
    for start in range(0, stripe, step):
        total = taps[0] * work[8 - half + start : 8 - half + start + step, :]
        for tap in range(1, count):
            begin = 8 - half + start + tap
            total = total + taps[tap] * work[begin : begin + step, :]
        out[start : start + step, :] = total.astype(BF16)


def filter_stripe(arriving, expiring, taps):
    stripe, samples = arriving.shape
    half = taps.shape[0] // 2
    axes = ("row", "col")
    count = lax.axis_size("row") * lax.axis_size("col")
    head = jnp.concatenate([arriving[:half], expiring[:half]], 1)
    tail = jnp.concatenate([arriving[-half:], expiring[-half:]], 1)
    above = lax.ppermute(tail, axes, [(i, i + 1) for i in range(count - 1)])
    below = lax.ppermute(head, axes, [(i + 1, i) for i in range(count - 1)])
    whole = pl.BlockSpec(memory_space=pltpu.VMEM)
    return pl.pallas_call(
        filter_kernel,
        in_specs=[pl.BlockSpec(memory_space=pltpu.SMEM), whole, whole, whole, whole],
        out_specs=whole,
        out_shape=jax.ShapeDtypeStruct((stripe, 2 * samples), BF16),
        scratch_shapes=[pltpu.VMEM((stripe + 16, 2 * samples), F32)],
        name="filter_stripe",
    )(taps, arriving, expiring, above, below)


def basis_kernel(block, gram, vectors, out, work):
    count = gram.shape[0]
    work[...] = gram[...]
    down = lax.broadcasted_iota(jnp.int32, (block, block), 0)
    across = lax.broadcasted_iota(jnp.int32, (block, block), 1)
    lane = lax.broadcasted_iota(jnp.int32, (1, count), 1)
    for start in range(0, count, block):
        end = start + block
        strip = work[start:end, :]
        square = strip[:, start:end]
        for j in range(block):
            row = square[j : j + 1, :]
            ratio = jnp.where(down[:, :1] > j, square[:, j : j + 1] / row[:, j : j + 1], 0.0)
            row = jnp.where(across[:1] == j, 1.0, row)
            square = jnp.where((across == j) & (down > j), 0.0, square) - ratio * row
        pivot = jnp.sum(jnp.where(down == across, square, 0.0), axis=1, keepdims=True)
        inverse = lax.rsqrt(pivot) * jnp.where(
            down > across, square, jnp.where(down == across, 1.0, 0.0)
        )
        strip = jnp.dot(inverse, strip, precision=HIGHEST, preferred_element_type=F32)
        pieces = [strip[:, :start]] if start else []
        pieces.append(inverse)
        if end < count:
            pieces.append(strip[:, end:])
        done = jnp.concatenate(pieces, axis=1)
        work[start:end, :] = done
        if end < count:
            change = lax.dot_general(
                strip[:, end:],
                done,
                (((0,), (0,)), ((), ())),
                precision=HIGHEST,
                preferred_element_type=F32,
            )
            old = jnp.where((lane >= start) & (lane < end), 0.0, work[end:, :])
            work[end:, :] = old - change
    down = lax.broadcasted_iota(jnp.int32, (count, count), 0)
    across = lax.broadcasted_iota(jnp.int32, (count, count), 1)
    factor = jnp.where(down >= across, work[...], 0.0)
    out[...] = lax.dot_general(
        vectors[...],
        factor,
        (((1,), (1,)), ((), ())),
        precision=HIGHEST,
        preferred_element_type=F32,
    )


def normalized(gram, vectors):
    count = gram.shape[0]
    return pl.pallas_call(
        functools.partial(basis_kernel, min(count, 64)),
        out_shape=jax.ShapeDtypeStruct(vectors.shape, F32),
        scratch_shapes=[pltpu.VMEM((count, count), F32)],
        compiler_params=pltpu.CompilerParams(vmem_limit_bytes=VMEM_LIMIT),
        name="normalized",
    )(gram, vectors)


def negated(data, samples):
    return jnp.concatenate([data[:, :samples], -data[:, samples:]], 1)


def inner(data, values):
    return lax.dot_general(data.astype(F32), values, (((0,), (0,)), ((), ())), precision=HIGHEST)


def correction(data, sums):
    high, low = halves(sums)
    return jnp.dot(data, high, preferred_element_type=F32) + jnp.dot(
        data, low, preferred_element_type=F32
    )


def shards(arriving, expiring, taps, covariance, vectors):
    stripe, samples = arriving.shape
    kept = vectors.shape[1]
    count_row, count_col = lax.axis_size("row"), lax.axis_size("col")
    channels = stripe * count_row * count_col
    planes = count_row // 2
    row_index, col_index = lax.axis_index("row"), lax.axis_index("col")
    z, x = row_index // 2, row_index % 2
    scale = 1.0 / samples

    own = jnp.concatenate(halves(vectors.T), 0)
    blocks = gather_pairs(own, "col")

    largest = largest_everywhere(jnp.max(jnp.abs(vectors)), planes)
    limit = 2.0 * 6.0 * channels
    grown = room(limit)
    size = power_of_two_for(largest[0, 0]) * grown

    filtered = filter_stripe(arriving, expiring, taps)
    moves = []
    for source in range(count_row * count_col):
        moves.append((source, (source % count_row) * count_col + source // count_row))
    other_filtered = lax.ppermute(filtered, ("row", "col"), moves)
    row_filtered = lax.all_gather(filtered, "col", axis=0, tiled=True)
    column_filtered = lax.all_gather(other_filtered, "row", axis=0, tiled=True)

    share = 1.0 / 16.0
    extra = turned(scatter_sum(inner(negated(filtered, samples), vectors) * share))
    received = []
    for j in reversed(range(planes)):
        if j == max(planes - 2, 0):
            extra = after(extra, other_filtered)
        send, keep = first_part(blocks, covariance, extra, z ^ j, x, col_index, stripe)
        half_sum = keep * size + swap((send * size).astype(F16), "row", 1).astype(F32)
        if j:
            received.append(swap(half_sum.astype(F16), "row", 2 * j))
        else:
            received.append(half_sum)
    total = received[-1]
    for part in received[:-1]:
        total = total + part.astype(F32)
    total = turned(total * (1.0 / grown))
    first_inner = gather_parts(total[stripe:] * (scale / share))
    first = total[:stripe] + correction(other_filtered, first_inner)

    grown = room(2.0 * (6.0 + 2.0 * (taps.shape[0] * 1.4 * 0.6) ** 2) * channels)
    own = (first * grown).astype(F16)
    far = [own] + [swap(own, "row", 2 * j) for j in range(1, planes)]
    partial, partials = None, []
    for j in range(planes):
        sent = far[j] if j < 2 else after(far[j], partials[j - 2])
        beside = swap(sent, "row", 1)
        entries = []
        for payload in (far[j], beside):
            own_entries = j == 0 and payload is own
            entries += halves(first if own_entries else payload.astype(F32) * (1.0 / grown))
        partial = second_part(covariance, entries, z ^ j, x, partial)
        partials.append(partial)
    second_inner = scatter_sum(inner(negated(other_filtered, samples), first) * scale)
    for mask, earlier in zip(bits_of("row"), partials):
        second_inner = second_inner + swap(after(second_inner, earlier), "row", mask)
    second_inner = gather_parts(second_inner)

    cells = partial.reshape(count_col, stripe, kept)
    for mask in bits_of("col"):
        cells = cells.reshape(cells.shape[0] // 2, 2, stripe, kept)
        upper = is_set("col", mask)
        mine = pick(upper, cells[:, 0], cells[:, 1])
        send = pick(upper, cells[:, 1], cells[:, 0])
        if mask == 1:
            cells = mine + swap(send, "col", mask)
        else:
            power = power_of_two_for(jnp.max(jnp.abs(send)))
            tail = jnp.full(send.shape[:1] + (16, kept), jnp.log2(power))
            payload = jnp.concatenate([send * (power * room(2.0)), tail], 1).astype(F16)
            other = swap(payload, "col", mask).astype(F32)
            power = lax.reduce_precision(jnp.exp2(-jnp.round(other[:, stripe : stripe + 1])), 8, 3)
            cells = mine + other[:, :stripe] * (power * (1.0 / room(2.0)))
    second = cells.reshape(stripe, kept) + correction(filtered, second_inner)
    gram_part = inner(second, second)

    signed_rows = negated(after(row_filtered, partials[max(planes - 3, 0)]), samples)
    updated = None
    for part in range(4):
        updated = update_part(
            covariance, signed_rows, column_filtered, part, 4, updated, scale
        )
    gram = gather_parts(sum_over_row(scatter_sum(gram_part))) / channels
    basis = normalized(after(gram, updated), second)
    return (updated, basis)


def solution(mesh):
    in_specs = (
        P(("row", "col"), None),
        P(("row", "col"), None),
        P(),
        P("row", "col"),
        P(("row", "col"), None),
    )
    out_specs = (P("row", "col"), P(("row", "col"), None))
    return jax.shard_map(shards, mesh=mesh, in_specs=in_specs, out_specs=out_specs, check_vma=False)
```

time: 689 us -> 350 us (0.51); the launches traced: 680 us -> 350 us
  waiting for transfers between devices: 461 us -> 106 us
  matrix products: 122 us -> 3.71 us
  Pallas kernels: 0 us -> 109 us
  starting transfers between devices: 3.93 us -> 81.9 us
  other arithmetic: 67.3 us -> 13 us
  between operations: 16 us -> 25.6 us
    all_gather x4 -> x2, waiting for transfers between devices: 212 us -> 0.02 us  [the longest x1 0.02 us: shards(): column_filtered = lax.all_gather(other_filtered, 'row', axis=0, tiled=True)]
    psum x1 -> x0, waiting for transfers between devices: 128 us -> none  [shards(): gram = lax.psum(local_gram, ('row', 'col')) / CH]
    reduce_scatter x2 -> x0, waiting for transfers between devices: 118 us -> none  [the longest x1 88.2 us: shards(): lax.psum_scatter(lax.dot_general(block, row_vectors, (((0,), (0,)), ((),...]
    dot_general x4 -> x7, matrix products: 120 us -> 3.71 us  [the longest x3 2.48 us: inner(): lax.dot_general(data.astype(F32), values, (((0,), (0,)), ((), ())), preci...]
    pallas_call x0 -> x16, Pallas kernels: none -> 109 us  [the longest x4 27.5 us: update_part(): pl.pallas_call(functools.partial(update_kernel, scale), grid=(steps,), in...]
    ppermute x2 -> x46, waiting for transfers between devices: 2.23 us -> 106 us  [the longest x43 104 us: swap(): lax.ppermute(cells, axis, [(i, i ^ mask) for i in range(lax.axis_size(axi...]
    ppermute x2 -> x46, starting transfers between devices: 3.65 us -> 81.7 us  [the longest x43 77.3 us: swap(): lax.ppermute(cells, axis, [(i, i ^ mask) for i in range(lax.axis_size(axi...]
    another operation x9 -> x4, other arithmetic: 53.7 us -> 0.3 us  [second_part(): jnp.stack([z * 2 + x, z * 2 + (1 - x)]).astype(jnp.int32)]
  transfers between devices with their start and end apart: 9 -> 48, of which waited for: 7 -> 22; matrix products, arithmetic and copies ran while one was open for 5% -> 6% of each run, Pallas kernels for 0% -> 13%
where the time goes in v1:
time: 350 us
  Pallas kernels  109 us (31%)
  waiting for transfers between devices  106 us (30%)
  starting transfers between devices  81.9 us (23%)
  between operations  25.6 us (7%)
  other arithmetic  13 us (4%)
  local copies, waits for them, and re-layouts  9.86 us (3%)
  matrix products  3.71 us (1%)
    ppermute x43, waiting for transfers between devices, swap(): lax.ppermute(cells, axis, [(i, i ^ mask) for i in range(lax.axis_size(axi...  104 us
    ppermute x43, starting transfers between devices, swap(): lax.ppermute(cells, axis, [(i, i ^ mask) for i in range(lax.axis_size(axi...  77.3 us
    pallas_call x4, Pallas kernels, update_part(): pl.pallas_call(functools.partial(update_kernel, scale), grid=(steps,), in...  27.5 us
    pallas_call x4, Pallas kernels, second_part(): pl.pallas_call(functools.partial(second_kernel, before is not None), grid...  27.3 us
    pallas_call x4, Pallas kernels, first_part(): pl.pallas_call(functools.partial(first_kernel, blocks), grid_spec=pltpu.P...  26.1 us
    pallas_call x1, Pallas kernels, normalized(): pl.pallas_call(functools.partial(basis_kernel, min(count, 64)), out_shape...  24.6 us
  transfers between devices with their start and end apart: 48, of which 22 were waited for; matrix products, arithmetic and copies ran while one was open for 6% of the time, Pallas kernels for 13%

profile of v1, /device:TPU:0, one launch (start us, length us, event | category | flops | bytes accessed | tf_op | source)
XLA Modules:
  0.0 349.6 jit_solution(2248942553132761378)
XLA Ops:
  8.0 2.4 collective-permute-start
  13.0 2.6 collective-permute-done.1.below
  16.2 3.4 filter_stripe.1
  21.5 2.5 collective-permute-start.2
  24.1 2.4 collective-permute-start.6
  27.8 2.7 collective-permute-start.9
  34.4 3.6 %collective-permute-start.5 = (bf16[512,512]{1,0:T(8,128)(2,1)S(1)}, bf16[512,512]{1,0:T(8,128)(2,1)S(1)}, u32[]{:S(2)}, u32[]{:S(2)}) collective-permute-start(bf16[512,512]{1,0:T(8,128)(2,1)S(1)} %pad_maximum_fusion.1.refs_0_), channel_id=1, source_target_pairs={{0,1},{1,0},{2,3},{3,2},{4,5},{5,4},{6,7},{7,6},{8,9},{9,8},{10,11... | collective-permute-start | bytes 1572872 | tf_op jit(solution)/shard_map/ppermute | solution.py:17
  38.0 2.9 collective-permute-start.3
  43.3 2.6 collective-permute-done.11
  49.2 3.6 %collective-permute-done.13 = f32[8,128]{1,0:T(8,128)} collective-permute-done((f32[8,128]{1,0:T(8,128)}, f32[8,128]{1,0:T(8,128)}, u32[]{:S(2)}, u32[]{:S(2)}) %collective-permute-start.13) | collective-permute-done | bytes 4128 | tf_op jit(solution)/shard_map/ppermute | solution.py:17
  57.9 6.5 %first_part.5 = (f32[256,640]{1,0:T(8,128)S(1)}, f32[256,640]{1,0:T(8,128)S(1)}) custom-call(s32[6]{0:T(128)S(1)} %stack.92.place, f32[256,128]{1,0:T(8,128)S(1)} %turned.2.extra, bf16[512,512]{1,0:T(8,128)(2,1)S(1)} %pad_maximum_fusion.1.refs_0_, bf16[512,512]{1,0:T(8,128)(2,1)S(1)} %collective-permute-done.5.refs_1_, ...), custom_call_target="tpu_custom_call" | custom-call | flops 3221225472 | bytes 8388608 | tf_op jit(solution)/shard_map/first_part/pallas_call | solution.py:137
  64.5 2.6 collective-permute-start.15
  67.1 6.5 %first_part.7 = (f32[256,640]{1,0:T(8,128)S(1)}, f32[256,640]{1,0:T(8,128)S(1)}) custom-call(s32[6]{0:T(128)S(1)} %stack.96.place, f32[256,128]{1,0:T(8,128)S(1)} %broadcast_add_fusion.6.extra, bf16[512,512]{1,0:T(8,128)(2,1)S(1)} %pad_maximum_fusion.1.refs_0_, bf16[512,512]{1,0:T(8,128)(2,1)S(1)} %collective-permute-done.5.refs_1_, ...), custom_call_target="tpu_custom_call" | custom-call | flops 3221225472 | bytes 8388608 | tf_op jit(solution)/shard_map/first_part/pallas_call | solution.py:137
  73.8 6.5 %first_part.6 = (f32[256,640]{1,0:T(8,128)S(1)}, f32[256,640]{1,0:T(8,128)S(1)}) custom-call(s32[6]{0:T(128)S(1)} %stack.95.place, f32[256,128]{1,0:T(8,128)S(1)} %broadcast_add_fusion.6.extra, bf16[512,512]{1,0:T(8,128)(2,1)S(1)} %pad_maximum_fusion.1.refs_0_, bf16[512,512]{1,0:T(8,128)(2,1)S(1)} %collective-permute-done.5.refs_1_, ...), custom_call_target="tpu_custom_call" | custom-call | flops 3221225472 | bytes 8388608 | tf_op jit(solution)/shard_map/first_part/pallas_call | solution.py:137
  80.3 6.5 %first_part.4 = (f32[256,640]{1,0:T(8,128)S(1)}, f32[256,640]{1,0:T(8,128)S(1)}) custom-call(s32[6]{0:T(128)S(1)} %stack.89.place, f32[256,128]{1,0:T(8,128)S(1)} %broadcast_add_fusion.6.extra, bf16[512,512]{1,0:T(8,128)(2,1)S(1)} %pad_maximum_fusion.1.refs_0_, bf16[512,512]{1,0:T(8,128)(2,1)S(1)} %collective-permute-done.5.refs_1_, ...), custom_call_target="tpu_custom_call" | custom-call | flops 3221225472 | bytes 8388608 | tf_op jit(solution)/shard_map/first_part/pallas_call | solution.py:137
  91.4 13.9 %collective-permute-start.20 = (f16[256,640]{1,0:T(8,128)(2,1)S(1)}, f16[256,640]{1,0:T(8,128)(2,1)}, u32[]{:S(2)}, u32[]{:S(2)}) collective-permute-start(f16[256,640]{1,0:T(8,128)(2,1)S(1)} %add_convert_fusion), channel_id=1, source_target_pairs={{0,8},{4,12},{8,0},{12,4},{16,24},{20,28},{24,16},{28,20},{1,9},{5... | collective-permute-start | bytes 983048 | tf_op jit(solution)/shard_map/ppermute | solution.py:17
  105.5 12.2 %collective-permute-start.18 = (f16[256,640]{1,0:T(8,128)(2,1)S(1)}, f16[256,640]{1,0:T(8,128)(2,1)S(1)}, u32[]{:S(2)}, u32[]{:S(2)}) collective-permute-start(f16[256,640]{1,0:T(8,128)(2,1)S(1)} %add_convert_fusion.1), channel_id=1, source_target_pairs={{0,16},{4,20},{8,24},{12,28},{16,0},{20,4},{24,8},{28,12},{1,17},{... | collective-permute-start | bytes 983048 | tf_op jit(solution)/shard_map/ppermute | solution.py:17
  118.0 12.3 %collective-permute-done.18 = f16[256,640]{1,0:T(8,128)(2,1)S(1)} collective-permute-done((f16[256,640]{1,0:T(8,128)(2,1)S(1)}, f16[256,640]{1,0:T(8,128)(2,1)S(1)}, u32[]{:S(2)}, u32[]{:S(2)}) %collective-permute-start.18) | collective-permute-done | bytes 327712 | tf_op jit(solution)/shard_map/ppermute | solution.py:17
  132.5 7.2 %collective-permute-done.21 = f32[128,256]{1,0:T(8,128)S(1)} collective-permute-done((f32[128,256]{1,0:T(8,128)S(1)}, f32[128,256]{1,0:T(8,128)S(1)}, u32[]{:S(2)}, u32[]{:S(2)}) %collective-permute-start.21) | collective-permute-done | bytes 131104 | tf_op jit(solution)/shard_map/ppermute | solution.py:17
  143.3 3.8 %collective-permute-start.26 = (f16[512,256]{1,0:T(8,128)(2,1)S(1)}, f16[512,256]{1,0:T(8,128)(2,1)S(1)}, u32[]{:S(2)}, u32[]{:S(2)}) collective-permute-start(f16[512,256]{1,0:T(8,128)(2,1)S(1)} %get-tuple-element.34), channel_id=1, source_target_pairs={{0,24},{4,28},{8,16},{12,20},{16,8},{20,12},{24,0},{28,4},{1,25},{... | collective-permute-start | bytes 786440 | tf_op jit(solution)/shard_map/ppermute | solution.py:17
  149.2 6.9 %collective-permute-done.25 = f16[512,256]{1,0:T(8,128)(2,1)S(1)} collective-permute-done((f16[512,256]{1,0:T(8,128)(2,1)S(1)}, f16[512,256]{1,0:T(8,128)(2,1)S(1)}, u32[]{:S(2)}, u32[]{:S(2)}) %collective-permute-start.25) | collective-permute-done | bytes 262176 | tf_op jit(solution)/shard_map/ppermute | solution.py:17
  156.2 6.8 %second_part.4.refs_6_ = f32[2048,256]{1,0:T(8,128)S(1)} custom-call(s32[2]{0:T(128)S(1)} %pad_add_fusion.1.place, f32[2048,4096]{1,0:T(8,128)} %refs_1_.7, f32[2048,4096]{1,0:T(8,128)} %refs_1_.7, bf16[512,256]{1,0:T(8,128)(2,1)S(1)} %get-tuple-element.33.refs_2_, bf16[512,256]{1,0:T(8,128)(2,1)S(1)} %get-tuple-element.32.refs_3_, ...), custom_call_target="tpu_custom_call" | custom-call | flops 3221225472 | bytes 8388608 | tf_op jit(solution)/shard_map/second_part/pallas_call | solution.py:225
  164.9 9.2 %collective-permute-done.28 = f16[512,256]{1,0:T(8,128)(2,1)S(1)} collective-permute-done((f16[512,256]{1,0:T(8,128)(2,1)S(1)}, f16[512,256]{1,0:T(8,128)(2,1)S(1)}, u32[]{:S(2)}, u32[]{:S(2)}) %collective-permute-start.28) | collective-permute-done | bytes 262176 | tf_op jit(solution)/shard_map/ppermute | solution.py:17
  174.1 2.3 collective-permute-start.29
  178.9 7.8 %collective-permute-done.24 = f16[512,256]{1,0:T(8,128)(2,1)S(1)} collective-permute-done((f16[512,256]{1,0:T(8,128)(2,1)S(1)}, f16[512,256]{1,0:T(8,128)(2,1)S(1)}, u32[]{:S(2)}, u32[]{:S(2)}) %collective-permute-start.24) | collective-permute-done | bytes 262176 | tf_op jit(solution)/shard_map/ppermute | solution.py:17
  186.8 6.9 %second_part.5.refs_6_ = f32[2048,256]{1,0:T(8,128)S(1)} custom-call(s32[2]{0:T(128)S(1)} %pad_add_fusion.place, f32[2048,4096]{1,0:T(8,128)} %refs_1_.7, f32[2048,4096]{1,0:T(8,128)} %refs_1_.7, bf16[512,256]{1,0:T(8,128)(2,1)S(1)} %get-tuple-element.62.refs_2_, bf16[512,256]{1,0:T(8,128)(2,1)S(1)} %get-tuple-element.61.refs_3_, ...), custom_call_target="tpu_custom_call" | custom-call | flops 3221225472 | bytes 8388608 | tf_op jit(solution)/shard_map/second_part/pallas_call | solution.py:225
  197.4 6.8 %second_part.6.refs_6_ = f32[2048,256]{1,0:T(8,128)S(1)} custom-call(s32[2]{0:T(128)S(1)} %pad_add_fusion.3.place, f32[2048,4096]{1,0:T(8,128)} %refs_1_.7, f32[2048,4096]{1,0:T(8,128)} %refs_1_.7, bf16[512,256]{1,0:T(8,128)(2,1)S(1)} %get-tuple-element.52.refs_2_, bf16[512,256]{1,0:T(8,128)(2,1)S(1)} %get-tuple-element.51.refs_3_, ...), custom_call_target="tpu_custom_call" | custom-call | flops 3221225472 | bytes 8388608 | tf_op jit(solution)/shard_map/second_part/pallas_call | solution.py:225
  204.2 4.2 %collective-permute-done.27 = f16[512,256]{1,0:T(8,128)(2,1)S(1)} collective-permute-done((f16[512,256]{1,0:T(8,128)(2,1)S(1)}, f16[512,256]{1,0:T(8,128)(2,1)S(1)}, u32[]{:S(2)}, u32[]{:S(2)}) %collective-permute-start.27) | collective-permute-done | bytes 262176 | tf_op jit(solution)/shard_map/ppermute | solution.py:17
  208.4 6.8 %second_part.7 = f32[2048,256]{1,0:T(8,128)S(1)} custom-call(s32[2]{0:T(128)S(1)} %pad_add_fusion.2.place, f32[2048,4096]{1,0:T(8,128)} %refs_1_.7, f32[2048,4096]{1,0:T(8,128)} %refs_1_.7, bf16[512,256]{1,0:T(8,128)(2,1)S(1)} %get-tuple-element.56.refs_2_, bf16[512,256]{1,0:T(8,128)(2,1)S(1)} %get-tuple-element.55.refs_3_, ...), custom_call_target="tpu_custom_call" | custom-call | flops 3221225472 | bytes 8388608 | tf_op jit(solution)/shard_map/second_part/pallas_call | solution.py:225
  215.5 3.7 %collective-permute-start.35 = (f32[128,256]{1,0:T(8,128)S(1)}, f32[128,256]{1,0:T(8,128)S(1)}, u32[]{:S(2)}, u32[]{:S(2)}) collective-permute-start(f32[128,256]{1,0:T(8,128)S(1)} %get-tuple-element.20), channel_id=1, source_target_pairs={{0,8},{4,12},{8,0},{12,4},{16,24},{20,28},{24,16},{28,20},{1,9},{5... | collective-permute-start | bytes 393224 | tf_op jit(solution)/shard_map/ppermute | solution.py:17
  221.0 9.4 %collective-permute-done.35 = f32[128,256]{1,0:T(8,128)S(1)} collective-permute-done((f32[128,256]{1,0:T(8,128)S(1)}, f32[128,256]{1,0:T(8,128)S(1)}, u32[]{:S(2)}, u32[]{:S(2)}) %collective-permute-start.35) | collective-permute-done | bytes 131104 | tf_op jit(solution)/shard_map/ppermute | solution.py:17
  230.4 2.5 collective-permute-start.36
  233.0 7.2 %collective-permute-done.36 = f32[128,256]{1,0:T(8,128)S(1)} collective-permute-done((f32[128,256]{1,0:T(8,128)S(1)}, f32[128,256]{1,0:T(8,128)S(1)}, u32[]{:S(2)}, u32[]{:S(2)}) %collective-permute-start.36) | collective-permute-done | bytes 131104 | tf_op jit(solution)/shard_map/ppermute | solution.py:17
  240.8 4.5 %collective-permute-done.37 = f32[128,256]{1,0:T(8,128)S(1)} collective-permute-done((f32[128,256]{1,0:T(8,128)S(1)}, f32[128,256]{1,0:T(8,128)S(1)}, u32[]{:S(2)}, u32[]{:S(2)}) %collective-permute-start.37) | collective-permute-done | bytes 131104 | tf_op jit(solution)/shard_map/ppermute | solution.py:17
  250.0 8.0 %collective-permute-done.31 = f16[1,528,256]{2,1,0:T(8,128)(2,1)S(1)} collective-permute-done((f16[1,528,256]{2,1,0:T(8,128)(2,1)S(1)}, f16[1,528,256]{2,1,0:T(8,128)(2,1)S(1)}, u32[]{:S(2)}, u32[]{:S(2)}) %collective-permute-start.31) | collective-permute-done | bytes 270368 | tf_op jit(solution)/shard_map/ppermute | solution.py:17
  261.5 3.8 %collective-permute-done.40 = f32[64,256]{1,0:T(8,128)S(1)} collective-permute-done((f32[64,256]{1,0:T(8,128)S(1)}, f32[64,256]{1,0:T(8,128)S(1)}, u32[]{:S(2)}, u32[]{:S(2)}) %collective-permute-start.40) | collective-permute-done | bytes 65568 | tf_op jit(solution)/shard_map/ppermute | solution.py:17
  265.3 2.2 collective-permute-start.41
  267.5 2.2 collective-permute-done.41
  270.1 4.0 %collective-permute-done.42 = f32[64,256]{1,0:T(8,128)S(1)} collective-permute-done((f32[64,256]{1,0:T(8,128)S(1)}, f32[64,256]{1,0:T(8,128)S(1)}, u32[]{:S(2)}, u32[]{:S(2)}) %collective-permute-start.42) | collective-permute-done | bytes 65568 | tf_op jit(solution)/shard_map/ppermute | solution.py:17
  274.1 2.1 collective-permute-start.43
  278.0 2.1 collective-permute-done.43
  280.6 3.8 %collective-permute-done.44 = f32[64,256]{1,0:T(8,128)S(1)} collective-permute-done((f32[64,256]{1,0:T(8,128)S(1)}, f32[64,256]{1,0:T(8,128)S(1)}, u32[]{:S(2)}, u32[]{:S(2)}) %collective-permute-start.44) | collective-permute-done | bytes 65568 | tf_op jit(solution)/shard_map/ppermute | solution.py:17
  285.9 2.2 copy-done
  288.1 6.9 %update_part.4.rest_0_ = f32[2048,4096]{1,0:T(8,128)} custom-call(f32[2048,4096]{1,0:T(8,128)} %refs_1_.7, bf16[2048,512]{1,0:T(8,128)(2,1)S(1)} %pad_maximum_fusion.rows, bf16[4096,512]{1,0:T(8,128)(2,1)S(1)} %copy-done), custom_call_target="tpu_custom_call" | custom-call | flops 2147483648 | bytes 16777216 | tf_op jit(solution)/shard_map/update_part/pallas_call | solution.py:260
  295.0 6.9 %update_part.5.rest_0_ = f32[2048,4096]{1,0:T(8,128)} custom-call(f32[2048,4096]{1,0:T(8,128)} %refs_1_.7, bf16[2048,512]{1,0:T(8,128)(2,1)S(1)} %pad_maximum_fusion.rows, bf16[4096,512]{1,0:T(8,128)(2,1)S(1)} %copy-done, f32[2048,4096]{1,0:T(8,128)} %update_part.4.rest_0_), custom_call_target="tpu_custom_call", output_to_operand_aliasing={{}: (3, {})} | custom-call | flops 2147483648 | bytes 16777216 | tf_op jit(solution)/shard_map/update_part/pallas_call | solution.py:260
  301.8 6.9 %update_part.6.rest_0_ = f32[2048,4096]{1,0:T(8,128)} custom-call(f32[2048,4096]{1,0:T(8,128)} %refs_1_.7, bf16[2048,512]{1,0:T(8,128)(2,1)S(1)} %pad_maximum_fusion.rows, bf16[4096,512]{1,0:T(8,128)(2,1)S(1)} %copy-done, f32[2048,4096]{1,0:T(8,128)} %update_part.5.rest_0_), custom_call_target="tpu_custom_call", output_to_operand_aliasing={{}: (3, {})} | custom-call | flops 2147483648 | bytes 16777216 | tf_op jit(solution)/shard_map/update_part/pallas_call | solution.py:260
  308.7 6.9 %update_part.7 = f32[2048,4096]{1,0:T(8,128)} custom-call(f32[2048,4096]{1,0:T(8,128)} %refs_1_.7, bf16[2048,512]{1,0:T(8,128)(2,1)S(1)} %pad_maximum_fusion.rows, bf16[4096,512]{1,0:T(8,128)(2,1)S(1)} %copy-done, f32[2048,4096]{1,0:T(8,128)} %update_part.6.rest_0_), custom_call_target="tpu_custom_call", output_to_operand_aliasing={{}: (3, {})} | custom-call | flops 2147483648 | bytes 16777216 | tf_op jit(solution)/shard_map/update_part/pallas_call | solution.py:260
  318.1 24.6 %normalized.1 = f32[512,256]{1,0:T(8,128)} custom-call(f32[256,256]{1,0:T(8,128)S(1)} %fusion.26.gram, f32[512,256]{1,0:T(8,128)S(1)} %fusion.14.vectors), custom_call_target="tpu_custom_call" | custom-call | tf_op jit(solution)/shard_map/normalized/pallas_call | solution.py:364
  (174 shorter events, 49.6 us)
Async XLA Ops:
  7.2 269.1 %all-gather.3.cloned.1.call-start = ((), (), s32[]{:S(2)}) async-start(), calls=%async_computation | async-start | bytes 2621440 | tf_op jit(solution)/shard_map/all_gather | solution.py:411
  8.0 4.9 %collective-permute-start = (f32[4,512]{1,0:T(4,128)S(1)}, f32[4,512]{1,0:T(4,128)S(1)}, u32[]{:S(2)}, u32[]{:S(2)}) collective-permute-start(f32[4,512]{1,0:T(4,128)S(1)} %pad_maximum_fusion.7), channel_id=1, source_target_pairs={{0,1},{1,2},{2,3},{3,4},{4,5},{5,6},{6,7},{7,8},{8,9},{9,10},{10,1... | collective-permute-start | bytes 24584 | tf_op jit(solution)/shard_map/ppermute | solution.py:301
  10.4 5.2 %collective-permute-start.1 = (f32[4,512]{1,0:T(4,128)S(1)}, f32[4,512]{1,0:T(4,128)S(1)}, u32[]{:S(2)}, u32[]{:S(2)}) collective-permute-start(f32[4,512]{1,0:T(4,128)S(1)} %pad_maximum_fusion.8), channel_id=1, source_target_pairs={{1,0},{2,1},{3,2},{4,3},{5,4},{6,5},{7,6},{8,7},{9,8},{10,9},{11,1... | collective-permute-start | bytes 24584 | tf_op jit(solution)/shard_map/ppermute | solution.py:302
  21.5 10.6 %collective-permute-start.2 = (f32[256,256]{1,0:T(8,128)S(1)}, f32[256,256]{1,0:T(8,128)}, u32[]{:S(2)}, u32[]{:S(2)}) collective-permute-start(f32[256,256]{1,0:T(8,128)S(1)} %slice_select_fusion.2), channel_id=1, source_target_pairs={{0,1},{1,0},{2,3},{3,2},{4,5},{5,4},{6,7},{7,6},{8,9},{9,8},{10,11... | collective-permute-start | bytes 786440 | tf_op jit(solution)/shard_map/ppermute | solution.py:17
  24.1 16.8 %collective-permute-start.6 = (bf16[512,512]{1,0:T(8,128)(2,1)S(1)}, bf16[512,512]{1,0:T(8,128)(2,1)S(1)}, u32[]{:S(2)}, u32[]{:S(2)}) collective-permute-start(bf16[512,512]{1,0:T(8,128)(2,1)S(1)} %pad_maximum_fusion.1.refs_0_), channel_id=1, source_target_pairs={{0,2},{1,3},{2,0},{3,1},{4,6},{5,7},{6,4},{7,5},{8,10},{9,11},{10,... | collective-permute-start | bytes 1572872 | tf_op jit(solution)/shard_map/ppermute | solution.py:17
  27.8 6.6 %collective-permute-start.9 = (f32[8,128]{1,0:T(8,128)S(1)}, f32[8,128]{1,0:T(8,128)S(1)}, u32[]{:S(2)}, u32[]{:S(2)}) collective-permute-start(f32[8,128]{1,0:T(8,128)S(1)} %broadcast_in_dim.4), channel_id=1, source_target_pairs={{0,16},{4,20},{8,24},{12,28},{16,0},{20,4},{24,8},{28,12},{1,17},{... | collective-permute-start | bytes 12296 | tf_op jit(solution)/shard_map/ppermute | solution.py:17
  30.5 7.5 %collective-permute-start.10 = (f32[8,128]{1,0:T(8,128)S(1)}, f32[8,128]{1,0:T(8,128)S(1)}, u32[]{:S(2)}, u32[]{:S(2)}) collective-permute-start(f32[8,128]{1,0:T(8,128)S(1)} %broadcast_in_dim.4), channel_id=1, source_target_pairs={{0,24},{4,28},{8,16},{12,20},{16,8},{20,12},{24,0},{28,4},{1,25},{... | collective-permute-start | bytes 12296 | tf_op jit(solution)/shard_map/ppermute | solution.py:17
  31.8 9.1 %collective-permute-start.8 = (f32[8,128]{1,0:T(8,128)S(1)}, f32[8,128]{1,0:T(8,128)}, u32[]{:S(2)}, u32[]{:S(2)}) collective-permute-start(f32[8,128]{1,0:T(8,128)S(1)} %broadcast_in_dim.4), channel_id=1, source_target_pairs={{0,8},{4,12},{8,0},{12,4},{16,24},{20,28},{24,16},{28,20},{1,9},{5... | collective-permute-start | bytes 12296 | tf_op jit(solution)/shard_map/ppermute | solution.py:17
  32.1 23.9 %collective-permute-start.4 = (bf16[512,512]{1,0:T(8,128)(2,1)S(1)}, bf16[512,512]{1,0:T(8,128)(2,1)S(1)}, u32[]{:S(2)}, u32[]{:S(2)}) collective-permute-start(bf16[512,512]{1,0:T(8,128)(2,1)S(1)} %copy-done.1), channel_id=1, source_target_pairs={{0,0},{1,4},{2,8},{3,12},{4,16},{5,20},{6,24},{7,28},{8,1},{9,5},{... | collective-permute-start | bytes 1572872 | tf_op jit(solution)/shard_map/ppermute | solution.py:410
  34.4 23.4 %collective-permute-start.5 = (bf16[512,512]{1,0:T(8,128)(2,1)S(1)}, bf16[512,512]{1,0:T(8,128)(2,1)S(1)}, u32[]{:S(2)}, u32[]{:S(2)}) collective-permute-start(bf16[512,512]{1,0:T(8,128)(2,1)S(1)} %pad_maximum_fusion.1.refs_0_), channel_id=1, source_target_pairs={{0,1},{1,0},{2,3},{3,2},{4,5},{5,4},{6,7},{7,6},{8,9},{9,8},{10,11... | collective-permute-start | bytes 1572872 | tf_op jit(solution)/shard_map/ppermute | solution.py:17
  38.0 17.9 %collective-permute-start.3 = (f32[128,256]{1,0:T(8,128)}, f32[128,256]{1,0:T(8,128)S(1)}, u32[]{:S(2)}, u32[]{:S(2)}) collective-permute-start(f32[128,256]{1,0:T(8,128)} %slice_select_fusion.5), channel_id=1, source_target_pairs={{0,2},{1,3},{2,0},{3,1},{4,6},{5,7},{6,4},{7,5},{8,10},{9,11},{10,... | collective-permute-start | bytes 393224 | tf_op jit(solution)/shard_map/ppermute | solution.py:17
  40.9 17.0 %collective-permute-start.7 = (bf16[512,512]{1,0:T(8,128)(2,1)S(1)}, bf16[512,512]{1,0:T(8,128)(2,1)S(1)}, u32[]{:S(2)}, u32[]{:S(2)}) collective-permute-start(bf16[512,512]{1,0:T(8,128)(2,1)S(1)} %collective-permute-done.6.refs_2_), channel_id=1, source_target_pairs={{0,1},{1,0},{2,3},{3,2},{4,5},{5,4},{6,7},{7,6},{8,9},{9,8},{10,11... | collective-permute-start | bytes 1572872 | tf_op jit(solution)/shard_map/ppermute | solution.py:17
  42.2 3.6 %collective-permute-start.11 = (f32[8,128]{1,0:T(8,128)S(1)}, f32[8,128]{1,0:T(8,128)S(1)}, u32[]{:S(2)}, u32[]{:S(2)}) collective-permute-start(f32[8,128]{1,0:T(8,128)S(1)} %maximum_maximum_fusion), channel_id=1, source_target_pairs={{0,4},{4,0},{8,12},{12,8},{16,20},{20,16},{24,28},{28,24},{1,5},{5... | collective-permute-start | bytes 12296 | tf_op jit(solution)/shard_map/ppermute | solution.py:17
  45.9 2.4 collective-permute-start.12
  48.9 3.9 %collective-permute-start.13 = (f32[8,128]{1,0:T(8,128)}, f32[8,128]{1,0:T(8,128)}, u32[]{:S(2)}, u32[]{:S(2)}) collective-permute-start(f32[8,128]{1,0:T(8,128)} %max.29), channel_id=1, source_target_pairs={{0,2},{1,3},{2,0},{3,1},{4,6},{5,7},{6,4},{7,5},{8,10},{9,11},{10,... | collective-permute-start | bytes 12296 | tf_op jit(solution)/shard_map/ppermute | solution.py:17
  64.5 24.6 %collective-permute-start.15 = (f16[256,640]{1,0:T(8,128)(2,1)S(1)}, f16[256,640]{1,0:T(8,128)(2,1)S(1)}, u32[]{:S(2)}, u32[]{:S(2)}) collective-permute-start(f16[256,640]{1,0:T(8,128)(2,1)S(1)} %multiply_convert_fusion.2), channel_id=1, source_target_pairs={{0,4},{4,0},{8,12},{12,8},{16,20},{20,16},{24,28},{28,24},{1,5},{5... | collective-permute-start | bytes 983048 | tf_op jit(solution)/shard_map/ppermute | solution.py:17
  73.7 17.6 %collective-permute-start.19 = (f16[256,640]{1,0:T(8,128)(2,1)S(1)}, f16[256,640]{1,0:T(8,128)(2,1)S(1)}, u32[]{:S(2)}, u32[]{:S(2)}) collective-permute-start(f16[256,640]{1,0:T(8,128)(2,1)S(1)} %multiply_convert_fusion), channel_id=1, source_target_pairs={{0,4},{4,0},{8,12},{12,8},{16,20},{20,16},{24,28},{28,24},{1,5},{5... | collective-permute-start | bytes 983048 | tf_op jit(solution)/shard_map/ppermute | solution.py:17
  87.0 30.9 %collective-permute-start.14 = (f16[256,640]{1,0:T(8,128)(2,1)S(1)}, f16[256,640]{1,0:T(8,128)(2,1)S(1)}, u32[]{:S(2)}, u32[]{:S(2)}) collective-permute-start(f16[256,640]{1,0:T(8,128)(2,1)S(1)} %multiply_convert_fusion.3), channel_id=1, source_target_pairs={{0,4},{4,0},{8,12},{12,8},{16,20},{20,16},{24,28},{28,24},{1,5},{5... | collective-permute-start | bytes 983048 | tf_op jit(solution)/shard_map/ppermute | solution.py:17
  89.1 16.3 %collective-permute-start.17 = (f16[256,640]{1,0:T(8,128)(2,1)S(1)}, f16[256,640]{1,0:T(8,128)(2,1)S(1)}, u32[]{:S(2)}, u32[]{:S(2)}) collective-permute-start(f16[256,640]{1,0:T(8,128)(2,1)S(1)} %multiply_convert_fusion.1), channel_id=1, source_target_pairs={{0,4},{4,0},{8,12},{12,8},{16,20},{20,16},{24,28},{28,24},{1,5},{5... | collective-permute-start | bytes 983048 | tf_op jit(solution)/shard_map/ppermute | solution.py:17
  89.2 28.7 %collective-permute-start.16 = (f16[256,640]{1,0:T(8,128)(2,1)S(1)}, f16[256,640]{1,0:T(8,128)(2,1)}, u32[]{:S(2)}, u32[]{:S(2)}) collective-permute-start(f16[256,640]{1,0:T(8,128)(2,1)S(1)} %add_convert_fusion.2), channel_id=1, source_target_pairs={{0,24},{4,28},{8,16},{12,20},{16,8},{20,12},{24,0},{28,4},{1,25},{... | collective-permute-start | bytes 983048 | tf_op jit(solution)/shard_map/ppermute | solution.py:17
  91.4 26.6 %collective-permute-start.20 = (f16[256,640]{1,0:T(8,128)(2,1)S(1)}, f16[256,640]{1,0:T(8,128)(2,1)}, u32[]{:S(2)}, u32[]{:S(2)}) collective-permute-start(f16[256,640]{1,0:T(8,128)(2,1)S(1)} %add_convert_fusion), channel_id=1, source_target_pairs={{0,8},{4,12},{8,0},{12,4},{16,24},{20,28},{24,16},{28,20},{1,9},{5... | collective-permute-start | bytes 983048 | tf_op jit(solution)/shard_map/ppermute | solution.py:17
  105.5 24.8 %collective-permute-start.18 = (f16[256,640]{1,0:T(8,128)(2,1)S(1)}, f16[256,640]{1,0:T(8,128)(2,1)S(1)}, u32[]{:S(2)}, u32[]{:S(2)}) collective-permute-start(f16[256,640]{1,0:T(8,128)(2,1)S(1)} %add_convert_fusion.1), channel_id=1, source_target_pairs={{0,16},{4,20},{8,24},{12,28},{16,0},{20,4},{24,8},{28,12},{1,17},{... | collective-permute-start | bytes 983048 | tf_op jit(solution)/shard_map/ppermute | solution.py:17
  117.7 168.2 %all-gather.5.cloned.1.call-start = ((), (), s32[]{:S(2)}) async-start(), calls=%async_computation.1 | async-start | bytes 4718592 | tf_op jit(solution)/shard_map/all_gather | solution.py:412
  131.9 7.8 %collective-permute-start.21 = (f32[128,256]{1,0:T(8,128)S(1)}, f32[128,256]{1,0:T(8,128)S(1)}, u32[]{:S(2)}, u32[]{:S(2)}) collective-permute-start(f32[128,256]{1,0:T(8,128)S(1)} %slice_multiply_fusion.1), channel_id=1, source_target_pairs={{0,2},{1,3},{2,0},{3,1},{4,6},{5,7},{6,4},{7,5},{8,10},{9,11},{10,... | collective-permute-start | bytes 393224 | tf_op jit(solution)/shard_map/ppermute | solution.py:17
  139.7 1.6 collective-permute-start.22
  142.8 5.9 %collective-permute-start.32 = (f32[256,256]{1,0:T(8,128)S(1)}, f32[256,256]{1,0:T(8,128)S(1)}, u32[]{:S(2)}, u32[]{:S(2)}) collective-permute-start(f32[256,256]{1,0:T(8,128)S(1)} %slice_select_fusion.1), channel_id=1, source_target_pairs={{0,1},{1,0},{2,3},{3,2},{4,5},{5,4},{6,7},{7,6},{8,9},{9,8},{10,11... | collective-permute-start | bytes 786440 | tf_op jit(solution)/shard_map/ppermute | solution.py:17
  143.2 30.8 %collective-permute-start.28 = (f16[512,256]{1,0:T(8,128)(2,1)S(1)}, f16[512,256]{1,0:T(8,128)(2,1)S(1)}, u32[]{:S(2)}, u32[]{:S(2)}) collective-permute-start(f16[512,256]{1,0:T(8,128)(2,1)S(1)} %get-tuple-element.34), channel_id=1, source_target_pairs={{0,16},{4,20},{8,24},{12,28},{16,0},{20,4},{24,8},{28,12},{1,17},{... | collective-permute-start | bytes 786440 | tf_op jit(solution)/shard_map/ppermute | solution.py:17
  143.3 33.4 %collective-permute-start.26 = (f16[512,256]{1,0:T(8,128)(2,1)S(1)}, f16[512,256]{1,0:T(8,128)(2,1)S(1)}, u32[]{:S(2)}, u32[]{:S(2)}) collective-permute-start(f16[512,256]{1,0:T(8,128)(2,1)S(1)} %get-tuple-element.34), channel_id=1, source_target_pairs={{0,24},{4,28},{8,16},{12,20},{16,8},{20,12},{24,0},{28,4},{1,25},{... | collective-permute-start | bytes 786440 | tf_op jit(solution)/shard_map/ppermute | solution.py:17
  147.1 9.0 %collective-permute-start.25 = (f16[512,256]{1,0:T(8,128)(2,1)S(1)}, f16[512,256]{1,0:T(8,128)(2,1)S(1)}, u32[]{:S(2)}, u32[]{:S(2)}) collective-permute-start(f16[512,256]{1,0:T(8,128)(2,1)S(1)} %get-tuple-element.34), channel_id=1, source_target_pairs={{0,4},{4,0},{8,12},{12,8},{16,20},{20,16},{24,28},{28,24},{1,5},{5... | collective-permute-start | bytes 786440 | tf_op jit(solution)/shard_map/ppermute | solution.py:17
  148.2 28.2 %collective-permute-start.23 = (f16[512,256]{1,0:T(8,128)(2,1)S(1)}, f16[512,256]{1,0:T(8,128)(2,1)S(1)}, u32[]{:S(2)}, u32[]{:S(2)}) collective-permute-start(f16[512,256]{1,0:T(8,128)(2,1)S(1)} %get-tuple-element.34), channel_id=1, source_target_pairs={{0,8},{4,12},{8,0},{12,4},{16,24},{20,28},{24,16},{28,20},{1,9},{5... | collective-permute-start | bytes 786440 | tf_op jit(solution)/shard_map/ppermute | solution.py:17
  148.8 28.0 %collective-permute-start.33 = (f32[128,256]{1,0:T(8,128)S(1)}, f32[128,256]{1,0:T(8,128)S(1)}, u32[]{:S(2)}, u32[]{:S(2)}) collective-permute-start(f32[128,256]{1,0:T(8,128)S(1)} %slice_select_fusion.4), channel_id=1, source_target_pairs={{0,2},{1,3},{2,0},{3,1},{4,6},{5,7},{6,4},{7,5},{8,10},{9,11},{10,... | collective-permute-start | bytes 393224 | tf_op jit(solution)/shard_map/ppermute | solution.py:17
  174.1 23.2 %collective-permute-start.29 = (f16[512,256]{1,0:T(8,128)(2,1)S(1)}, f16[512,256]{1,0:T(8,128)(2,1)S(1)}, u32[]{:S(2)}, u32[]{:S(2)}) collective-permute-start(f16[512,256]{1,0:T(8,128)(2,1)S(1)} %broadcast_add_fusion.1), channel_id=1, source_target_pairs={{0,4},{4,0},{8,12},{12,8},{16,20},{20,16},{24,28},{28,24},{1,5},{5... | collective-permute-start | bytes 786440 | tf_op jit(solution)/shard_map/ppermute | solution.py:17
  176.4 10.3 %collective-permute-start.24 = (f16[512,256]{1,0:T(8,128)(2,1)S(1)}, f16[512,256]{1,0:T(8,128)(2,1)S(1)}, u32[]{:S(2)}, u32[]{:S(2)}) collective-permute-start(f16[512,256]{1,0:T(8,128)(2,1)S(1)} %collective-permute-done.23), channel_id=1, source_target_pairs={{0,4},{4,0},{8,12},{12,8},{16,20},{20,16},{24,28},{28,24},{1,5},{5... | collective-permute-start | bytes 786440 | tf_op jit(solution)/shard_map/ppermute | solution.py:17
  176.8 38.6 %collective-permute-start.34 = (f32[128,256]{1,0:T(8,128)S(1)}, f32[128,256]{1,0:T(8,128)S(1)}, u32[]{:S(2)}, u32[]{:S(2)}) collective-permute-start(f32[128,256]{1,0:T(8,128)S(1)} %get-tuple-element.22), channel_id=1, source_target_pairs={{0,4},{4,0},{8,12},{12,8},{16,20},{20,16},{24,28},{28,24},{1,5},{5... | collective-permute-start | bytes 393224 | tf_op jit(solution)/shard_map/ppermute | solution.py:17
  195.6 12.7 %collective-permute-start.27 = (f16[512,256]{1,0:T(8,128)(2,1)S(1)}, f16[512,256]{1,0:T(8,128)(2,1)S(1)}, u32[]{:S(2)}, u32[]{:S(2)}) collective-permute-start(f16[512,256]{1,0:T(8,128)(2,1)S(1)} %broadcast_add_fusion.2), channel_id=1, source_target_pairs={{0,4},{4,0},{8,12},{12,8},{16,20},{20,16},{24,28},{28,24},{1,5},{5... | collective-permute-start | bytes 786440 | tf_op jit(solution)/shard_map/ppermute | solution.py:17
  215.4 30.1 %collective-permute-start.30 = (f32[2,512,256]{2,1,0:T(8,128)S(1)}, f32[2,512,256]{2,1,0:T(8,128)S(1)}, u32[]{:S(2)}, u32[]{:S(2)}) collective-permute-start(f32[2,512,256]{2,1,0:T(8,128)S(1)} %select_bitcast_fusion), channel_id=1, source_target_pairs={{0,1},{1,0},{2,3},{3,2},{4,5},{5,4},{6,7},{7,6},{8,9},{9,8},{10,11... | collective-permute-start | bytes 3145736 | tf_op jit(solution)/shard_map/ppermute | solution.py:17
  215.5 14.9 %collective-permute-start.35 = (f32[128,256]{1,0:T(8,128)S(1)}, f32[128,256]{1,0:T(8,128)S(1)}, u32[]{:S(2)}, u32[]{:S(2)}) collective-permute-start(f32[128,256]{1,0:T(8,128)S(1)} %get-tuple-element.20), channel_id=1, source_target_pairs={{0,8},{4,12},{8,0},{12,4},{16,24},{20,28},{24,16},{28,20},{1,9},{5... | collective-permute-start | bytes 393224 | tf_op jit(solution)/shard_map/ppermute | solution.py:17
  230.4 9.7 %collective-permute-start.36 = (f32[128,256]{1,0:T(8,128)S(1)}, f32[128,256]{1,0:T(8,128)S(1)}, u32[]{:S(2)}, u32[]{:S(2)}) collective-permute-start(f32[128,256]{1,0:T(8,128)S(1)} %get-tuple-element.18), channel_id=1, source_target_pairs={{0,16},{4,20},{8,24},{12,28},{16,0},{20,4},{24,8},{28,12},{1,17},{... | collective-permute-start | bytes 393224 | tf_op jit(solution)/shard_map/ppermute | solution.py:17
  240.2 5.1 %collective-permute-start.37 = (f32[128,256]{1,0:T(8,128)S(1)}, f32[128,256]{1,0:T(8,128)S(1)}, u32[]{:S(2)}, u32[]{:S(2)}) collective-permute-start(f32[128,256]{1,0:T(8,128)S(1)} %add.204), channel_id=1, source_target_pairs={{0,2},{1,3},{2,0},{3,1},{4,6},{5,7},{6,4},{7,5},{8,10},{9,11},{10,... | collective-permute-start | bytes 393224 | tf_op jit(solution)/shard_map/ppermute | solution.py:17
  245.4 4.3 %collective-permute-start.38 = (f32[256,256]{1,0:T(8,128)S(1)}, f32[256,256]{1,0:T(8,128)S(1)}, u32[]{:S(2)}, u32[]{:S(2)}) collective-permute-start(f32[256,256]{1,0:T(8,128)S(1)} %pad_maximum_fusion.5), channel_id=1, source_target_pairs={{0,1},{1,0},{2,3},{3,2},{4,5},{5,4},{6,7},{7,6},{8,9},{9,8},{10,11... | collective-permute-start | bytes 786440 | tf_op jit(solution)/shard_map/ppermute | solution.py:17
  249.1 8.9 %collective-permute-start.31 = (f16[1,528,256]{2,1,0:T(8,128)(2,1)S(1)}, f16[1,528,256]{2,1,0:T(8,128)(2,1)S(1)}, u32[]{:S(2)}, u32[]{:S(2)}) collective-permute-start(f16[1,528,256]{2,1,0:T(8,128)(2,1)S(1)} %concatenate.46), channel_id=1, source_target_pairs={{0,2},{1,3},{2,0},{3,1},{4,6},{5,7},{6,4},{7,5},{8,10},{9,11},{10,... | collective-permute-start | bytes 811016 | tf_op jit(solution)/shard_map/ppermute | solution.py:17
  259.5 1.4 collective-permute-start.39
  260.9 4.3 %collective-permute-start.40 = (f32[64,256]{1,0:T(8,128)S(1)}, f32[64,256]{1,0:T(8,128)S(1)}, u32[]{:S(2)}, u32[]{:S(2)}) collective-permute-start(f32[64,256]{1,0:T(8,128)S(1)} %slice_select_fusion.6), channel_id=1, source_target_pairs={{0,2},{1,3},{2,0},{3,1},{4,6},{5,7},{6,4},{7,5},{8,10},{9,11},{10,... | collective-permute-start | bytes 196616 | tf_op jit(solution)/shard_map/ppermute | solution.py:17
  265.3 4.5 %collective-permute-start.41 = (f32[64,256]{1,0:T(8,128)S(1)}, f32[64,256]{1,0:T(8,128)S(1)}, u32[]{:S(2)}, u32[]{:S(2)}) collective-permute-start(f32[64,256]{1,0:T(8,128)S(1)} %select_add_fusion.5), channel_id=1, source_target_pairs={{0,4},{4,0},{8,12},{12,8},{16,20},{20,16},{24,28},{28,24},{1,5},{5... | collective-permute-start | bytes 196616 | tf_op jit(solution)/shard_map/ppermute | solution.py:17
  269.8 4.3 %collective-permute-start.42 = (f32[64,256]{1,0:T(8,128)S(1)}, f32[64,256]{1,0:T(8,128)S(1)}, u32[]{:S(2)}, u32[]{:S(2)}) collective-permute-start(f32[64,256]{1,0:T(8,128)S(1)} %add.209), channel_id=1, source_target_pairs={{0,8},{4,12},{8,0},{12,4},{16,24},{20,28},{24,16},{28,20},{1,9},{5... | collective-permute-start | bytes 196616 | tf_op jit(solution)/shard_map/ppermute | solution.py:17
  274.1 5.9 %collective-permute-start.43 = (f32[64,256]{1,0:T(8,128)S(1)}, f32[64,256]{1,0:T(8,128)S(1)}, u32[]{:S(2)}, u32[]{:S(2)}) collective-permute-start(f32[64,256]{1,0:T(8,128)S(1)} %add.210), channel_id=1, source_target_pairs={{0,16},{4,20},{8,24},{12,28},{16,0},{20,4},{24,8},{28,12},{1,17},{... | collective-permute-start | bytes 196616 | tf_op jit(solution)/shard_map/ppermute | solution.py:17
  280.1 4.3 %collective-permute-start.44 = (f32[64,256]{1,0:T(8,128)S(1)}, f32[64,256]{1,0:T(8,128)S(1)}, u32[]{:S(2)}, u32[]{:S(2)}) collective-permute-start(f32[64,256]{1,0:T(8,128)S(1)} %add.211), channel_id=1, source_target_pairs={{0,2},{1,3},{2,0},{3,1},{4,6},{5,7},{6,4},{7,5},{8,10},{9,11},{10,... | collective-permute-start | bytes 196616 | tf_op jit(solution)/shard_map/ppermute | solution.py:17
  284.4 1.4 collective-permute-start.45
  (8 other events, 51.7 us)
Sparse Core Ops, SparseCore 0:
  117.8 23.4 all-gather.2
  144.0 91.2 all-gather.4

commit v2 on v1

--- a/solution.py
+++ b/solution.py
@@ -95,9 +95,10 @@
     return high, (values - high.astype(F32)).astype(BF16)
 
 
-def first_kernel(blocks, place, extra, *refs):
+def first_kernel(blocks, place, *refs):
+    extra, refs = refs[0], refs[1:]
     vectors, tiles = refs[:blocks], refs[blocks : 2 * blocks]
-    send, keep = refs[2 * blocks :]
+    send, keep = refs[-2:]
     count = send.shape[0]
     total = None
     for part, tile in zip(vectors, tiles):
@@ -118,7 +119,7 @@
         keep[:, total.shape[1] :] = extra[...]
 
 
-def first_part(vectors, tile, extra, z, x, column, stripe):
+def first_part(vectors, tile, extra, z, x, column, stripe, waits=()):
     rows = tile.shape[0]
     blocks = len(vectors)
     count = vectors[0].shape[0] // 2
@@ -141,7 +142,8 @@
             grid=(2,),
             in_specs=[pl.BlockSpec((count, width), lambda i, p: (0, 0))]
             + [pl.BlockSpec((2 * count, depth), lambda i, p: (0, 0))] * blocks
-            + [pl.BlockSpec((depth, stripe), rows_of(i)) for i in range(blocks)],
+            + [pl.BlockSpec((depth, stripe), rows_of(i)) for i in range(blocks)]
+            + [pl.BlockSpec(memory_space=pl.ANY)] * len(waits),
             out_specs=[pl.BlockSpec(shape, lambda i, p: (0, 0))] * 2,
         ),
         out_shape=[jax.ShapeDtypeStruct(shape, F32)] * 2,
@@ -150,7 +152,7 @@
             flops=12 * count * rows * stripe, bytes_accessed=8 * rows * stripe, transcendentals=0
         ),
         name="first_part",
-    )(place, extra, *vectors, *([tile] * blocks))
+    )(place, extra, *vectors, *([tile] * blocks), *waits)
 
 
 def first_part_plain(vectors, tile, extra, z, x, column, stripe):
@@ -207,7 +209,7 @@
     out[...] = total
 
 
-def second_part(tile, entries, z, x, before):
+def second_part(tile, entries, z, x, before, waits=()):
     rows = tile.shape[0]
     depth, count = entries[0].shape
     if depth % 128:
@@ -222,6 +224,8 @@
     if before is not None:
         specs.append(total)
         operands.append(before)
+    specs += [pl.BlockSpec(memory_space=pl.ANY)] * len(waits)
+    operands += waits
     return pl.pallas_call(
         functools.partial(second_kernel, before is not None),
         grid_spec=pltpu.PrefetchScalarGridSpec(
@@ -240,10 +244,11 @@
     change = lax.dot_general(
         rows[...], columns[...], (((1,), (1,)), ((), ())), preferred_element_type=F32
     )
-    rest[-1][...] = tile[...] + change * scale
-
-
-def update_part(tile, rows, columns, part, parts, before, scale):
+    rest[-2][...] = tile[...] + change * scale
+    rest[-1][...] = jnp.zeros(rest[-1].shape, F32)
+
+
+def update_part(tile, rows, columns, part, parts, before, scale, kept, waits):
     height, width = tile.shape
     depth = rows.shape[1]
     high = min(height // parts, 256)
@@ -257,12 +262,20 @@
     if before is not None:
         specs.append(pl.BlockSpec(memory_space=pl.ANY))
         operands.append(before)
+    specs += [pl.BlockSpec(memory_space=pl.ANY)] * len(waits)
+    operands += waits
     return pl.pallas_call(
         functools.partial(update_kernel, scale),
         grid=(steps,),
         in_specs=specs,
-        out_specs=pl.BlockSpec((high, width), lambda i: (part * steps + i, 0)),
-        out_shape=jax.ShapeDtypeStruct((height, width), F32),
+        out_specs=[
+            pl.BlockSpec((high, width), lambda i: (part * steps + i, 0)),
+            pl.BlockSpec((1, kept), lambda i: (0, 0)),
+        ],
+        out_shape=[
+            jax.ShapeDtypeStruct((height, width), F32),
+            jax.ShapeDtypeStruct((1, kept), F32),
+        ],
         input_output_aliases={} if before is None else {3: 0},
         compiler_params=pltpu.CompilerParams(vmem_limit_bytes=VMEM_LIMIT),
         cost_estimate=pl.CostEstimate(
@@ -415,17 +428,16 @@
     extra = turned(scatter_sum(inner(negated(filtered, samples), vectors) * share))
     received = []
     for j in reversed(range(planes)):
-        if j == max(planes - 2, 0):
-            extra = after(extra, other_filtered)
-        send, keep = first_part(blocks, covariance, extra, z ^ j, x, col_index, stripe)
+        waits = {0: [other_filtered], 3: received[:1]}.get(len(received), [])
+        send, keep = first_part(blocks, covariance, extra, z ^ j, x, col_index, stripe, waits)
         half_sum = keep * size + swap((send * size).astype(F16), "row", 1).astype(F32)
         if j:
-            received.append(swap(half_sum.astype(F16), "row", 2 * j))
+            received.append(swap(half_sum.astype(F16), "row", 2 * j).astype(F32))
         else:
             received.append(half_sum)
     total = received[-1]
     for part in received[:-1]:
-        total = total + part.astype(F32)
+        total = total + part
     total = turned(total * (1.0 / grown))
     first_inner = gather_parts(total[stripe:] * (scale / share))
     first = total[:stripe] + correction(other_filtered, first_inner)
@@ -441,12 +453,21 @@
         for payload in (far[j], beside):
             own_entries = j == 0 and payload is own
             entries += halves(first if own_entries else payload.astype(F32) * (1.0 / grown))
-        partial = second_part(covariance, entries, z ^ j, x, partial)
+        waits = [column_filtered] if j == 1 else []
+        partial = second_part(covariance, entries, z ^ j, x, partial, waits)
         partials.append(partial)
     second_inner = scatter_sum(inner(negated(other_filtered, samples), first) * scale)
     for mask, earlier in zip(bits_of("row"), partials):
         second_inner = second_inner + swap(after(second_inner, earlier), "row", mask)
-    second_inner = gather_parts(second_inner)
+
+    signed_rows = negated(row_filtered, samples)
+    updated, written = None, []
+    for part, waits in enumerate(([partial], [partial], [partial], [partial])):
+        updated, row = update_part(
+            covariance, signed_rows, column_filtered, part, 4, updated, scale, kept, waits
+        )
+        written.append(row)
+    second_inner = gather_parts(second_inner + written[0])
 
     cells = partial.reshape(count_col, stripe, kept)
     for mask in bits_of("col"):
@@ -463,17 +484,14 @@
             other = swap(payload, "col", mask).astype(F32)
             power = lax.reduce_precision(jnp.exp2(-jnp.round(other[:, stripe : stripe + 1])), 8, 3)
             cells = mine + other[:, :stripe] * (power * (1.0 / room(2.0)))
-    second = cells.reshape(stripe, kept) + correction(filtered, second_inner)
-    gram_part = inner(second, second)
-
-    signed_rows = negated(after(row_filtered, partials[max(planes - 3, 0)]), samples)
-    updated = None
-    for part in range(4):
-        updated = update_part(
-            covariance, signed_rows, column_filtered, part, 4, updated, scale
-        )
-    gram = gather_parts(sum_over_row(scatter_sum(gram_part))) / channels
-    basis = normalized(after(gram, updated), second)
+    second = cells.reshape(stripe, kept) + correction(filtered, second_inner) + written[1]
+
+    gram = scatter_sum(inner(second, second))
+    for i, mask in enumerate(bits_of("row")):
+        gram = gram + swap(gram, "row", mask)
+        if i < 2:
+            gram = gram + written[2 + i]
+    basis = normalized(gather_parts(gram) / channels, second)
     return (updated, basis)
 
 

time: 350 us -> 337 us (0.963)
  waiting for transfers between devices: 106 us -> 86.9 us
  other arithmetic: 13 us -> 19.5 us
    ppermute x43, waiting for transfers between devices: 104 us -> 83 us  [swap(): lax.ppermute(cells, axis, [(i, i ^ mask) for i in range(lax.axis_size(axi...]
    unnamed x17 -> x41, local copies, waits for them, and re-layouts: 4.05 us -> 7.71 us
  transfers between devices with their start and end apart: 48 -> 48, of which waited for: 22 -> 19; matrix products, arithmetic and copies ran while one was open for 6% -> 7% of each run, Pallas kernels for 13% -> 25%
where the time goes in v2:
time: 337 us; the launch traced here: 336 us
  Pallas kernels  111 us (33%)
  waiting for transfers between devices  86.9 us (26%)
  starting transfers between devices  78.7 us (23%)
  between operations  23.3 us (7%)
  other arithmetic  19.5 us (6%)
  local copies, waits for them, and re-layouts  11.7 us (3%)
  matrix products  5.07 us (2%)
    ppermute x43, waiting for transfers between devices, swap(): lax.ppermute(cells, axis, [(i, i ^ mask) for i in range(lax.axis_size(axi...  83 us
    ppermute x43, starting transfers between devices, swap(): lax.ppermute(cells, axis, [(i, i ^ mask) for i in range(lax.axis_size(axi...  74.3 us
    pallas_call x4, Pallas kernels, update_part(): pl.pallas_call(functools.partial(update_kernel, scale), grid=(steps,), in...  28.5 us
    pallas_call x4, Pallas kernels, second_part(): pl.pallas_call(functools.partial(second_kernel, before is not None), grid...  27.8 us
    pallas_call x4, Pallas kernels, first_part(): pl.pallas_call(functools.partial(first_kernel, blocks), grid_spec=pltpu.P...  26.5 us
    pallas_call x1, Pallas kernels, normalized(): pl.pallas_call(functools.partial(basis_kernel, min(count, 64)), out_shape...  24.6 us
    unnamed x41, local copies, waits for them, and re-layouts  7.71 us
  transfers between devices with their start and end apart: 48, of which 19 were waited for; matrix products, arithmetic and copies ran while one was open for 7% of the time, Pallas kernels for 25%

profile of v2, /device:TPU:0, one launch (start us, length us, event | category | flops | bytes accessed | tf_op | source)
XLA Modules:
  0.0 336.4 jit_solution(2423604240099074615)
XLA Ops:
  8.0 2.4 collective-permute-start
  11.7 3.9 %collective-permute-done.1.below = f32[4,512]{1,0:T(4,128)S(1)} collective-permute-done((f32[4,512]{1,0:T(4,128)S(1)}, f32[4,512]{1,0:T(4,128)S(1)}, u32[]{:S(2)}, u32[]{:S(2)}) %collective-permute-start.1) | collective-permute-done | bytes 8224 | tf_op jit(solution)/shard_map/ppermute | solution.py:315
  16.2 3.4 %filter_stripe.1 = bf16[512,512]{1,0:T(8,128)(2,1)} custom-call(f32[9]{0:T(128)} %taps.1, f32[512,256]{1,0:T(8,128)} %arriving.1, f32[512,256]{1,0:T(8,128)} %expiring.1, f32[4,512]{1,0:T(4,128)} %copy-done.18, f32[4,512]{1,0:T(4,128)} %copy-done.19), custom_call_target="tpu_custom_call" | custom-call | tf_op jit(solution)/shard_map/filter_stripe/pallas_call | solution.py:317
  20.0 2.4 collective-permute-start.6
  23.3 2.2 collective-permute-start.3
  26.8 2.7 collective-permute-start.9
  32.7 2.1 collective-permute-done.6.refs_3_
  34.8 7.5 %collective-permute-start.7 = (bf16[512,512]{1,0:T(8,128)(2,1)S(1)}, bf16[512,512]{1,0:T(8,128)(2,1)S(1)}, u32[]{:S(2)}, u32[]{:S(2)}) collective-permute-start(bf16[512,512]{1,0:T(8,128)(2,1)S(1)} %collective-permute-done.6.refs_3_), channel_id=1, source_target_pairs={{0,1},{1,0},{2,3},{3,2},{4,5},{5,4},{6,7},{7,6},{8,9},{9,8},{10,11... | collective-permute-start | bytes 1572872 | tf_op jit(solution)/shard_map/ppermute | solution.py:17
  43.0 3.4 %collective-permute-start.4 = (f32[128,256]{1,0:T(8,128)}, f32[128,256]{1,0:T(8,128)S(1)}, u32[]{:S(2)}, u32[]{:S(2)}) collective-permute-start(f32[128,256]{1,0:T(8,128)} %slice_select_fusion.5), channel_id=1, source_target_pairs={{0,2},{1,3},{2,0},{3,1},{4,6},{5,7},{6,4},{7,5},{8,10},{9,11},{10,... | collective-permute-start | bytes 393224 | tf_op jit(solution)/shard_map/ppermute | solution.py:17
  47.7 3.6 %collective-permute-done.11 = f32[8,128]{1,0:T(8,128)S(1)} collective-permute-done((f32[8,128]{1,0:T(8,128)S(1)}, f32[8,128]{1,0:T(8,128)S(1)}, u32[]{:S(2)}, u32[]{:S(2)}) %collective-permute-start.11) | collective-permute-done | bytes 4128 | tf_op jit(solution)/shard_map/ppermute | solution.py:17
  53.4 3.6 %collective-permute-done.13 = f32[8,128]{1,0:T(8,128)} collective-permute-done((f32[8,128]{1,0:T(8,128)}, f32[8,128]{1,0:T(8,128)}, u32[]{:S(2)}, u32[]{:S(2)}) %collective-permute-start.13) | collective-permute-done | bytes 4128 | tf_op jit(solution)/shard_map/ppermute | solution.py:17
  62.3 6.7 %first_part.4 = (f32[256,640]{1,0:T(8,128)S(1)}, f32[256,640]{1,0:T(8,128)S(1)}) custom-call(s32[6]{0:T(128)S(1)} %stack.90.place, f32[256,128]{1,0:T(8,128)S(1)} %turned.2.refs_0_, bf16[512,512]{1,0:T(8,128)(2,1)S(1)} %pad_maximum_fusion.1.refs_1_, bf16[512,512]{1,0:T(8,128)(2,1)S(1)} %collective-permute-done.5.refs_2_, ...), custom_call_target="tpu_custom_call" | custom-call | flops 3221225472 | bytes 8388608 | tf_op jit(solution)/shard_map/first_part/pallas_call | solution.py:138
  70.1 6.5 %first_part.6 = (f32[256,640]{1,0:T(8,128)S(1)}, f32[256,640]{1,0:T(8,128)S(1)}) custom-call(s32[6]{0:T(128)S(1)} %stack.93.place, f32[256,128]{1,0:T(8,128)S(1)} %turned.2.refs_0_, bf16[512,512]{1,0:T(8,128)(2,1)S(1)} %pad_maximum_fusion.1.refs_1_, bf16[512,512]{1,0:T(8,128)(2,1)S(1)} %collective-permute-done.5.refs_2_, ...), custom_call_target="tpu_custom_call" | custom-call | flops 3221225472 | bytes 8388608 | tf_op jit(solution)/shard_map/first_part/pallas_call | solution.py:138
  77.9 6.8 %first_part.7 = (f32[256,640]{1,0:T(8,128)S(1)}, f32[256,640]{1,0:T(8,128)S(1)}) custom-call(s32[6]{0:T(128)S(1)} %stack.96.place, f32[256,128]{1,0:T(8,128)S(1)} %turned.2.refs_0_, bf16[512,512]{1,0:T(8,128)(2,1)S(1)} %pad_maximum_fusion.1.refs_1_, bf16[512,512]{1,0:T(8,128)(2,1)S(1)} %collective-permute-done.5.refs_2_, ...), custom_call_target="tpu_custom_call" | custom-call | flops 3221225472 | bytes 8388608 | tf_op jit(solution)/shard_map/first_part/pallas_call | solution.py:138
  85.7 3.8 %collective-permute-start.15 = (f16[256,640]{1,0:T(8,128)(2,1)S(1)}, f16[256,640]{1,0:T(8,128)(2,1)S(1)}, u32[]{:S(2)}, u32[]{:S(2)}) collective-permute-start(f16[256,640]{1,0:T(8,128)(2,1)S(1)} %add_convert_fusion.2), channel_id=1, source_target_pairs={{0,24},{4,28},{8,16},{12,20},{16,8},{20,12},{24,0},{28,4},{1,25},{... | collective-permute-start | bytes 983048 | tf_op jit(solution)/shard_map/ppermute | solution.py:17
  89.6 14.8 %collective-permute-start.18 = (f16[256,640]{1,0:T(8,128)(2,1)S(1)}, f16[256,640]{1,0:T(8,128)(2,1)S(1)}, u32[]{:S(2)}, u32[]{:S(2)}) collective-permute-start(f16[256,640]{1,0:T(8,128)(2,1)S(1)} %add_convert_fusion.1), channel_id=1, source_target_pairs={{0,16},{4,20},{8,24},{12,28},{16,0},{20,4},{24,8},{28,12},{1,17},{... | collective-permute-start | bytes 983048 | tf_op jit(solution)/shard_map/ppermute | solution.py:17
  104.5 4.4 %collective-permute-start.20 = (f16[256,640]{1,0:T(8,128)(2,1)S(1)}, f16[256,640]{1,0:T(8,128)(2,1)S(1)}, u32[]{:S(2)}, u32[]{:S(2)}) collective-permute-start(f16[256,640]{1,0:T(8,128)(2,1)S(1)} %add_convert_fusion), channel_id=1, source_target_pairs={{0,8},{4,12},{8,0},{12,4},{16,24},{20,28},{24,16},{28,20},{1,9},{5... | collective-permute-start | bytes 983048 | tf_op jit(solution)/shard_map/ppermute | solution.py:17
  109.0 6.5 %first_part.5 = (f32[256,640]{1,0:T(8,128)S(1)}, f32[256,640]{1,0:T(8,128)S(1)}) custom-call(s32[6]{0:T(128)S(1)} %stack.89.place, f32[256,128]{1,0:T(8,128)S(1)} %turned.2.refs_0_, bf16[512,512]{1,0:T(8,128)(2,1)S(1)} %pad_maximum_fusion.1.refs_1_, bf16[512,512]{1,0:T(8,128)(2,1)S(1)} %collective-permute-done.5.refs_2_, ...), custom_call_target="tpu_custom_call" | custom-call | flops 3221225472 | bytes 8388608 | tf_op jit(solution)/shard_map/first_part/pallas_call | solution.py:138
  116.3 24.6 %collective-permute-done.18 = f16[256,640]{1,0:T(8,128)(2,1)S(1)} collective-permute-done((f16[256,640]{1,0:T(8,128)(2,1)S(1)}, f16[256,640]{1,0:T(8,128)(2,1)S(1)}, u32[]{:S(2)}, u32[]{:S(2)}) %collective-permute-start.18) | collective-permute-done | bytes 327712 | tf_op jit(solution)/shard_map/ppermute | solution.py:17
  141.4 1.6 collective-permute-start.21
  142.9 3.5 %collective-permute-done.21 = f32[128,256]{1,0:T(8,128)S(1)} collective-permute-done((f32[128,256]{1,0:T(8,128)S(1)}, f32[128,256]{1,0:T(8,128)S(1)}, u32[]{:S(2)}, u32[]{:S(2)}) %collective-permute-start.21) | collective-permute-done | bytes 131104 | tf_op jit(solution)/shard_map/ppermute | solution.py:17
  150.0 7.1 %collective-permute-start.28 = (f16[512,256]{1,0:T(8,128)(2,1)S(1)}, f16[512,256]{1,0:T(8,128)(2,1)S(1)}, u32[]{:S(2)}, u32[]{:S(2)}) collective-permute-start(f16[512,256]{1,0:T(8,128)(2,1)S(1)} %get-tuple-element.50), channel_id=1, source_target_pairs={{0,16},{4,20},{8,24},{12,28},{16,0},{20,4},{24,8},{28,12},{1,17},{... | collective-permute-start | bytes 786440 | tf_op jit(solution)/shard_map/ppermute | solution.py:17
  157.1 1.7 collective-permute-start.26
  158.8 1.9 collective-permute-start.23
  162.2 3.2 collective-permute-done.26
  165.4 6.8 %second_part.4.refs_6_ = f32[2048,256]{1,0:T(8,128)S(1)} custom-call(s32[2]{0:T(128)S(1)} %pad_add_fusion.2.place, f32[2048,4096]{1,0:T(8,128)} %tile.7, f32[2048,4096]{1,0:T(8,128)} %tile.7, bf16[512,256]{1,0:T(8,128)(2,1)S(1)} %get-tuple-element.49.refs_2_, bf16[512,256]{1,0:T(8,128)(2,1)S(1)} %get-tuple-element.48.refs_3_, ...), custom_call_target="tpu_custom_call" | custom-call | flops 3221225472 | bytes 8388608 | tf_op jit(solution)/shard_map/second_part/pallas_call | solution.py:229
  174.1 9.2 %collective-permute-done.28 = f16[512,256]{1,0:T(8,128)(2,1)S(1)} collective-permute-done((f16[512,256]{1,0:T(8,128)(2,1)S(1)}, f16[512,256]{1,0:T(8,128)(2,1)S(1)}, u32[]{:S(2)}, u32[]{:S(2)}) %collective-permute-start.28) | collective-permute-done | bytes 262176 | tf_op jit(solution)/shard_map/ppermute | solution.py:17
  184.1 1.6 collective-permute-done.24
  189.5 8.8 %collective-permute-done.25 = f16[512,256]{1,0:T(8,128)(2,1)S(1)} collective-permute-done((f16[512,256]{1,0:T(8,128)(2,1)S(1)}, f16[512,256]{1,0:T(8,128)(2,1)S(1)}, u32[]{:S(2)}, u32[]{:S(2)}) %collective-permute-start.25) | collective-permute-done | bytes 262176 | tf_op jit(solution)/shard_map/ppermute | solution.py:17
  200.2 1.7 fusion.38
  203.4 2.2 copy-done
  208.4 7.1 %second_part.5.refs_6_ = f32[2048,256]{1,0:T(8,128)S(1)} custom-call(s32[2]{0:T(128)S(1)} %pad_add_fusion.1.place, f32[2048,4096]{1,0:T(8,128)} %tile.7, f32[2048,4096]{1,0:T(8,128)} %tile.7, bf16[512,256]{1,0:T(8,128)(2,1)S(1)} %copy-done.8, bf16[512,256]{1,0:T(8,128)(2,1)S(1)} %get-tuple-element.75.refs_3_, bf16[512,256]{1,0:T(8,128)(2,1)S(1)} %copy-done.12, ...), custom_call_target="tpu_custom_call" | custom-call | flops 3221225472 | bytes 8388608 | tf_op jit(solution)/shard_map/second_part/pallas_call | solution.py:229
  219.1 6.8 %second_part.6.refs_6_ = f32[2048,256]{1,0:T(8,128)S(1)} custom-call(s32[2]{0:T(128)S(1)} %pad_add_fusion.3.place, f32[2048,4096]{1,0:T(8,128)} %tile.7, f32[2048,4096]{1,0:T(8,128)} %tile.7, bf16[512,256]{1,0:T(8,128)(2,1)S(1)} %get-tuple-element.68.refs_2_, bf16[512,256]{1,0:T(8,128)(2,1)S(1)} %get-tuple-element.67.refs_3_, ...), custom_call_target="tpu_custom_call" | custom-call | flops 3221225472 | bytes 8388608 | tf_op jit(solution)/shard_map/second_part/pallas_call | solution.py:229
  227.8 7.1 %second_part.7.rest_0_.rest_1_ = f32[2048,256]{1,0:T(8,128)S(1)} custom-call(s32[2]{0:T(128)S(1)} %pad_add_fusion.place, f32[2048,4096]{1,0:T(8,128)} %tile.7, f32[2048,4096]{1,0:T(8,128)} %tile.7, bf16[512,256]{1,0:T(8,128)(2,1)S(1)} %get-tuple-element.78.refs_2_, bf16[512,256]{1,0:T(8,128)(2,1)S(1)} %get-tuple-element.77.refs_3_, ...), custom_call_target="tpu_custom_call" | custom-call | flops 3221225472 | bytes 8388608 | tf_op jit(solution)/shard_map/second_part/pallas_call | solution.py:229
  235.2 2.2 collective-permute-start.36
  237.4 7.1 %update_part.4 = (f32[2048,4096]{1,0:T(8,128)}, f32[1,256]{1,0:T(1,128)S(1)}) custom-call(f32[2048,4096]{1,0:T(8,128)} %tile.7, bf16[2048,512]{1,0:T(8,128)(2,1)S(1)} %copy-done.3, bf16[4096,512]{1,0:T(8,128)(2,1)S(1)} %copy-done.1, f32[2048,256]{1,0:T(8,128)S(1)} %second_part.7.rest_0_.rest_1_), custom_call_target="tpu_custom_call" | custom-call | flops 2147483648 | bytes 16777216 | tf_op jit(solution)/shard_map/update_part/pallas_call | solution.py:267
  246.3 7.1 %update_part.5 = (f32[2048,4096]{1,0:T(8,128)}, f32[1,256]{1,0:T(1,128)S(1)}) custom-call(f32[2048,4096]{1,0:T(8,128)} %tile.7, bf16[2048,512]{1,0:T(8,128)(2,1)S(1)} %copy-done.3, bf16[4096,512]{1,0:T(8,128)(2,1)S(1)} %copy-done.1, f32[2048,4096]{1,0:T(8,128)} %get-tuple-element.26.rest_0_, ...), custom_call_target="tpu_custom_call", output_to_operand_aliasing={{0}: (3, {})} | custom-call | flops 2147483648 | bytes 16777216 | tf_op jit(solution)/shard_map/update_part/pallas_call | solution.py:267
  254.9 2.0 abs_reduce_fusion
  261.8 7.9 %collective-permute-done.31 = f16[1,528,256]{2,1,0:T(8,128)(2,1)S(1)} collective-permute-done((f16[1,528,256]{2,1,0:T(8,128)(2,1)S(1)}, f16[1,528,256]{2,1,0:T(8,128)(2,1)S(1)}, u32[]{:S(2)}, u32[]{:S(2)}) %collective-permute-start.31) | collective-permute-done | bytes 270368 | tf_op jit(solution)/shard_map/ppermute | solution.py:17
  269.8 1.7 fusion.15.vectors
  274.7 3.6 %collective-permute-done.40 = f32[64,256]{1,0:T(8,128)S(1)} collective-permute-done((f32[64,256]{1,0:T(8,128)S(1)}, f32[64,256]{1,0:T(8,128)S(1)}, u32[]{:S(2)}, u32[]{:S(2)}) %collective-permute-start.40) | collective-permute-done | bytes 65568 | tf_op jit(solution)/shard_map/ppermute | solution.py:17
  279.0 7.1 %update_part.6 = (f32[2048,4096]{1,0:T(8,128)}, f32[1,256]{1,0:T(1,128)S(1)}) custom-call(f32[2048,4096]{1,0:T(8,128)} %tile.7, bf16[2048,512]{1,0:T(8,128)(2,1)S(1)} %copy-done.4, bf16[4096,512]{1,0:T(8,128)(2,1)S(1)} %copy-done.2, f32[2048,4096]{1,0:T(8,128)} %get-tuple-element.27.rest_0_, ...), custom_call_target="tpu_custom_call", output_to_operand_aliasing={{0}: (3, {})} | custom-call | flops 2147483648 | bytes 16777216 | tf_op jit(solution)/shard_map/update_part/pallas_call | solution.py:267
  286.7 7.1 %update_part.7 = (f32[2048,4096]{1,0:T(8,128)}, f32[1,256]{1,0:T(1,128)S(1)}) custom-call(f32[2048,4096]{1,0:T(8,128)} %tile.7, bf16[2048,512]{1,0:T(8,128)(2,1)S(1)} %copy-done.4, bf16[4096,512]{1,0:T(8,128)(2,1)S(1)} %copy-done.2, f32[2048,4096]{1,0:T(8,128)} %get-tuple-element.28.rest_0_, ...), custom_call_target="tpu_custom_call", output_to_operand_aliasing={{0}: (3, {})} | custom-call | flops 2147483648 | bytes 16777216 | tf_op jit(solution)/shard_map/update_part/pallas_call | solution.py:267
  293.8 2.0 collective-permute-start.43
  295.9 3.2 collective-permute-done.43
  299.1 1.8 collective-permute-start.44
  300.9 2.5 collective-permute-done.44
  304.9 24.6 %normalized.1 = f32[512,256]{1,0:T(8,128)} custom-call(f32[256,256]{1,0:T(8,128)S(1)} %maximum_multiply_fusion.gram, f32[512,256]{1,0:T(8,128)S(1)} %fusion.15.vectors), custom_call_target="tpu_custom_call" | custom-call | tf_op jit(solution)/shard_map/normalized/pallas_call | solution.py:377
  (195 shorter events, 51.6 us)
Async XLA Ops:
  7.2 193.0 %all-gather.3.cloned.1.call-start = ((), (), s32[]{:S(2)}) async-start(), calls=%async_computation | async-start | bytes 2621440 | tf_op jit(solution)/shard_map/all_gather | solution.py:424
  8.0 3.7 %collective-permute-start = (f32[4,512]{1,0:T(4,128)S(1)}, f32[4,512]{1,0:T(4,128)S(1)}, u32[]{:S(2)}, u32[]{:S(2)}) collective-permute-start(f32[4,512]{1,0:T(4,128)S(1)} %pad_maximum_fusion.7), channel_id=1, source_target_pairs={{0,1},{1,2},{2,3},{3,4},{4,5},{5,6},{6,7},{7,8},{8,9},{9,10},{10,1... | collective-permute-start | bytes 24584 | tf_op jit(solution)/shard_map/ppermute | solution.py:314
  10.4 5.2 %collective-permute-start.1 = (f32[4,512]{1,0:T(4,128)S(1)}, f32[4,512]{1,0:T(4,128)S(1)}, u32[]{:S(2)}, u32[]{:S(2)}) collective-permute-start(f32[4,512]{1,0:T(4,128)S(1)} %pad_maximum_fusion.8), channel_id=1, source_target_pairs={{1,0},{2,1},{3,2},{4,3},{5,4},{6,5},{7,6},{8,7},{9,8},{10,9},{11,1... | collective-permute-start | bytes 24584 | tf_op jit(solution)/shard_map/ppermute | solution.py:315
  19.7 183.7 %all-gather.5.cloned.1.call-start = ((), (), s32[]{:S(2)}) async-start(), calls=%async_computation.1 | async-start | bytes 4718592 | tf_op jit(solution)/shard_map/all_gather | solution.py:425
  20.0 14.8 %collective-permute-start.6 = (bf16[512,512]{1,0:T(8,128)(2,1)S(1)}, bf16[512,512]{1,0:T(8,128)(2,1)S(1)}, u32[]{:S(2)}, u32[]{:S(2)}) collective-permute-start(bf16[512,512]{1,0:T(8,128)(2,1)S(1)} %pad_maximum_fusion.1.refs_1_), channel_id=1, source_target_pairs={{0,2},{1,3},{2,0},{3,1},{4,6},{5,7},{6,4},{7,5},{8,10},{9,11},{10,... | collective-permute-start | bytes 1572872 | tf_op jit(solution)/shard_map/ppermute | solution.py:17
  23.3 7.7 %collective-permute-start.3 = (f32[256,256]{1,0:T(8,128)S(1)}, f32[256,256]{1,0:T(8,128)}, u32[]{:S(2)}, u32[]{:S(2)}) collective-permute-start(f32[256,256]{1,0:T(8,128)S(1)} %slice_select_fusion.2), channel_id=1, source_target_pairs={{0,1},{1,0},{2,3},{3,2},{4,5},{5,4},{6,7},{7,6},{8,9},{9,8},{10,11... | collective-permute-start | bytes 786440 | tf_op jit(solution)/shard_map/ppermute | solution.py:17
  26.8 5.3 %collective-permute-start.9 = (f32[8,128]{1,0:T(8,128)S(1)}, f32[8,128]{1,0:T(8,128)S(1)}, u32[]{:S(2)}, u32[]{:S(2)}) collective-permute-start(f32[8,128]{1,0:T(8,128)S(1)} %broadcast_in_dim.4), channel_id=1, source_target_pairs={{0,16},{4,20},{8,24},{12,28},{16,0},{20,4},{24,8},{28,12},{1,17},{... | collective-permute-start | bytes 12296 | tf_op jit(solution)/shard_map/ppermute | solution.py:17
  29.4 13.6 %collective-permute-start.10 = (f32[8,128]{1,0:T(8,128)S(1)}, f32[8,128]{1,0:T(8,128)S(1)}, u32[]{:S(2)}, u32[]{:S(2)}) collective-permute-start(f32[8,128]{1,0:T(8,128)S(1)} %broadcast_in_dim.4), channel_id=1, source_target_pairs={{0,24},{4,28},{8,16},{12,20},{16,8},{20,12},{24,0},{28,4},{1,25},{... | collective-permute-start | bytes 12296 | tf_op jit(solution)/shard_map/ppermute | solution.py:17
  30.8 15.6 %collective-permute-start.8 = (f32[8,128]{1,0:T(8,128)S(1)}, f32[8,128]{1,0:T(8,128)}, u32[]{:S(2)}, u32[]{:S(2)}) collective-permute-start(f32[8,128]{1,0:T(8,128)S(1)} %broadcast_in_dim.4), channel_id=1, source_target_pairs={{0,8},{4,12},{8,0},{12,4},{16,24},{20,28},{24,16},{28,20},{1,9},{5... | collective-permute-start | bytes 12296 | tf_op jit(solution)/shard_map/ppermute | solution.py:17
  31.0 30.3 %collective-permute-start.5 = (bf16[512,512]{1,0:T(8,128)(2,1)S(1)}, bf16[512,512]{1,0:T(8,128)(2,1)S(1)}, u32[]{:S(2)}, u32[]{:S(2)}) collective-permute-start(bf16[512,512]{1,0:T(8,128)(2,1)S(1)} %pad_maximum_fusion.1.refs_1_), channel_id=1, source_target_pairs={{0,1},{1,0},{2,3},{3,2},{4,5},{5,4},{6,7},{7,6},{8,9},{9,8},{10,11... | collective-permute-start | bytes 1572872 | tf_op jit(solution)/shard_map/ppermute | solution.py:17
  32.0 28.4 %collective-permute-start.2 = (bf16[512,512]{1,0:T(8,128)(2,1)S(1)}, bf16[512,512]{1,0:T(8,128)(2,1)S(1)}, u32[]{:S(2)}, u32[]{:S(2)}) collective-permute-start(bf16[512,512]{1,0:T(8,128)(2,1)S(1)} %copy-done.13), channel_id=1, source_target_pairs={{0,0},{1,4},{2,8},{3,12},{4,16},{5,20},{6,24},{7,28},{8,1},{9,5},{... | collective-permute-start | bytes 1572872 | tf_op jit(solution)/shard_map/ppermute | solution.py:423
  34.8 26.4 %collective-permute-start.7 = (bf16[512,512]{1,0:T(8,128)(2,1)S(1)}, bf16[512,512]{1,0:T(8,128)(2,1)S(1)}, u32[]{:S(2)}, u32[]{:S(2)}) collective-permute-start(bf16[512,512]{1,0:T(8,128)(2,1)S(1)} %collective-permute-done.6.refs_3_), channel_id=1, source_target_pairs={{0,1},{1,0},{2,3},{3,2},{4,5},{5,4},{6,7},{7,6},{8,9},{9,8},{10,11... | collective-permute-start | bytes 1572872 | tf_op jit(solution)/shard_map/ppermute | solution.py:17
  43.0 17.3 %collective-permute-start.4 = (f32[128,256]{1,0:T(8,128)}, f32[128,256]{1,0:T(8,128)S(1)}, u32[]{:S(2)}, u32[]{:S(2)}) collective-permute-start(f32[128,256]{1,0:T(8,128)} %slice_select_fusion.5), channel_id=1, source_target_pairs={{0,2},{1,3},{2,0},{3,1},{4,6},{5,7},{6,4},{7,5},{8,10},{9,11},{10,... | collective-permute-start | bytes 393224 | tf_op jit(solution)/shard_map/ppermute | solution.py:17
  47.7 3.6 %collective-permute-start.11 = (f32[8,128]{1,0:T(8,128)S(1)}, f32[8,128]{1,0:T(8,128)S(1)}, u32[]{:S(2)}, u32[]{:S(2)}) collective-permute-start(f32[8,128]{1,0:T(8,128)S(1)} %maximum_maximum_fusion), channel_id=1, source_target_pairs={{0,4},{4,0},{8,12},{12,8},{16,20},{20,16},{24,28},{28,24},{1,5},{5... | collective-permute-start | bytes 12296 | tf_op jit(solution)/shard_map/ppermute | solution.py:17
  51.3 1.2 collective-permute-start.12
  53.1 3.9 %collective-permute-start.13 = (f32[8,128]{1,0:T(8,128)}, f32[8,128]{1,0:T(8,128)}, u32[]{:S(2)}, u32[]{:S(2)}) collective-permute-start(f32[8,128]{1,0:T(8,128)} %max.29), channel_id=1, source_target_pairs={{0,2},{1,3},{2,0},{3,1},{4,6},{5,7},{6,4},{7,5},{8,10},{9,11},{10,... | collective-permute-start | bytes 12296 | tf_op jit(solution)/shard_map/ppermute | solution.py:17
  69.1 16.4 %collective-permute-start.14 = (f16[256,640]{1,0:T(8,128)(2,1)S(1)}, f16[256,640]{1,0:T(8,128)(2,1)S(1)}, u32[]{:S(2)}, u32[]{:S(2)}) collective-permute-start(f16[256,640]{1,0:T(8,128)(2,1)S(1)} %multiply_convert_fusion.3), channel_id=1, source_target_pairs={{0,4},{4,0},{8,12},{12,8},{16,20},{20,16},{24,28},{28,24},{1,5},{5... | collective-permute-start | bytes 983048 | tf_op jit(solution)/shard_map/ppermute | solution.py:17
  76.7 12.8 %collective-permute-start.17 = (f16[256,640]{1,0:T(8,128)(2,1)S(1)}, f16[256,640]{1,0:T(8,128)(2,1)S(1)}, u32[]{:S(2)}, u32[]{:S(2)}) collective-permute-start(f16[256,640]{1,0:T(8,128)(2,1)S(1)} %multiply_convert_fusion.1), channel_id=1, source_target_pairs={{0,4},{4,0},{8,12},{12,8},{16,20},{20,16},{24,28},{28,24},{1,5},{5... | collective-permute-start | bytes 983048 | tf_op jit(solution)/shard_map/ppermute | solution.py:17
  84.7 19.6 %collective-permute-start.19 = (f16[256,640]{1,0:T(8,128)(2,1)S(1)}, f16[256,640]{1,0:T(8,128)(2,1)S(1)}, u32[]{:S(2)}, u32[]{:S(2)}) collective-permute-start(f16[256,640]{1,0:T(8,128)(2,1)S(1)} %multiply_convert_fusion), channel_id=1, source_target_pairs={{0,4},{4,0},{8,12},{12,8},{16,20},{20,16},{24,28},{28,24},{1,5},{5... | collective-permute-start | bytes 983048 | tf_op jit(solution)/shard_map/ppermute | solution.py:17
  85.7 23.2 %collective-permute-start.15 = (f16[256,640]{1,0:T(8,128)(2,1)S(1)}, f16[256,640]{1,0:T(8,128)(2,1)S(1)}, u32[]{:S(2)}, u32[]{:S(2)}) collective-permute-start(f16[256,640]{1,0:T(8,128)(2,1)S(1)} %add_convert_fusion.2), channel_id=1, source_target_pairs={{0,24},{4,28},{8,16},{12,20},{16,8},{20,12},{24,0},{28,4},{1,25},{... | collective-permute-start | bytes 983048 | tf_op jit(solution)/shard_map/ppermute | solution.py:17
  89.6 51.3 %collective-permute-start.18 = (f16[256,640]{1,0:T(8,128)(2,1)S(1)}, f16[256,640]{1,0:T(8,128)(2,1)S(1)}, u32[]{:S(2)}, u32[]{:S(2)}) collective-permute-start(f16[256,640]{1,0:T(8,128)(2,1)S(1)} %add_convert_fusion.1), channel_id=1, source_target_pairs={{0,16},{4,20},{8,24},{12,28},{16,0},{20,4},{24,8},{28,12},{1,17},{... | collective-permute-start | bytes 983048 | tf_op jit(solution)/shard_map/ppermute | solution.py:17
  104.5 36.4 %collective-permute-start.20 = (f16[256,640]{1,0:T(8,128)(2,1)S(1)}, f16[256,640]{1,0:T(8,128)(2,1)S(1)}, u32[]{:S(2)}, u32[]{:S(2)}) collective-permute-start(f16[256,640]{1,0:T(8,128)(2,1)S(1)} %add_convert_fusion), channel_id=1, source_target_pairs={{0,8},{4,12},{8,0},{12,4},{16,24},{20,28},{24,16},{28,20},{1,9},{5... | collective-permute-start | bytes 983048 | tf_op jit(solution)/shard_map/ppermute | solution.py:17
  115.6 25.3 %collective-permute-start.16 = (f16[256,640]{1,0:T(8,128)(2,1)S(1)}, f16[256,640]{1,0:T(8,128)(2,1)S(1)}, u32[]{:S(2)}, u32[]{:S(2)}) collective-permute-start(f16[256,640]{1,0:T(8,128)(2,1)S(1)} %multiply_convert_fusion.2), channel_id=1, source_target_pairs={{0,4},{4,0},{8,12},{12,8},{16,20},{20,16},{24,28},{28,24},{1,5},{5... | collective-permute-start | bytes 983048 | tf_op jit(solution)/shard_map/ppermute | solution.py:17
  141.4 5.0 %collective-permute-start.21 = (f32[128,256]{1,0:T(8,128)S(1)}, f32[128,256]{1,0:T(8,128)S(1)}, u32[]{:S(2)}, u32[]{:S(2)}) collective-permute-start(f32[128,256]{1,0:T(8,128)S(1)} %slice_multiply_fusion.1), channel_id=1, source_target_pairs={{0,2},{1,3},{2,0},{3,1},{4,6},{5,7},{6,4},{7,5},{8,10},{9,11},{10,... | collective-permute-start | bytes 393224 | tf_op jit(solution)/shard_map/ppermute | solution.py:17
  146.5 1.6 collective-permute-start.22
  149.5 11.2 %collective-permute-start.32 = (f32[256,256]{1,0:T(8,128)S(1)}, f32[256,256]{1,0:T(8,128)S(1)}, u32[]{:S(2)}, u32[]{:S(2)}) collective-permute-start(f32[256,256]{1,0:T(8,128)S(1)} %slice_select_fusion.1), channel_id=1, source_target_pairs={{0,1},{1,0},{2,3},{3,2},{4,5},{5,4},{6,7},{7,6},{8,9},{9,8},{10,11... | collective-permute-start | bytes 786440 | tf_op jit(solution)/shard_map/ppermute | solution.py:17
  150.0 33.4 %collective-permute-start.28 = (f16[512,256]{1,0:T(8,128)(2,1)S(1)}, f16[512,256]{1,0:T(8,128)(2,1)S(1)}, u32[]{:S(2)}, u32[]{:S(2)}) collective-permute-start(f16[512,256]{1,0:T(8,128)(2,1)S(1)} %get-tuple-element.50), channel_id=1, source_target_pairs={{0,16},{4,20},{8,24},{12,28},{16,0},{20,4},{24,8},{28,12},{1,17},{... | collective-permute-start | bytes 786440 | tf_op jit(solution)/shard_map/ppermute | solution.py:17
  157.1 8.3 %collective-permute-start.26 = (f16[512,256]{1,0:T(8,128)(2,1)S(1)}, f16[512,256]{1,0:T(8,128)(2,1)S(1)}, u32[]{:S(2)}, u32[]{:S(2)}) collective-permute-start(f16[512,256]{1,0:T(8,128)(2,1)S(1)} %get-tuple-element.50), channel_id=1, source_target_pairs={{0,4},{4,0},{8,12},{12,8},{16,20},{20,16},{24,28},{28,24},{1,5},{5... | collective-permute-start | bytes 786440 | tf_op jit(solution)/shard_map/ppermute | solution.py:17
  158.8 26.9 %collective-permute-start.24 = (f16[512,256]{1,0:T(8,128)(2,1)S(1)}, f16[512,256]{1,0:T(8,128)(2,1)S(1)}, u32[]{:S(2)}, u32[]{:S(2)}) collective-permute-start(f16[512,256]{1,0:T(8,128)(2,1)S(1)} %get-tuple-element.50), channel_id=1, source_target_pairs={{0,8},{4,12},{8,0},{12,4},{16,24},{20,28},{24,16},{28,20},{1,9},{5... | collective-permute-start | bytes 786440 | tf_op jit(solution)/shard_map/ppermute | solution.py:17
  158.8 28.4 %collective-permute-start.23 = (f16[512,256]{1,0:T(8,128)(2,1)S(1)}, f16[512,256]{1,0:T(8,128)(2,1)S(1)}, u32[]{:S(2)}, u32[]{:S(2)}) collective-permute-start(f16[512,256]{1,0:T(8,128)(2,1)S(1)} %get-tuple-element.50), channel_id=1, source_target_pairs={{0,24},{4,28},{8,16},{12,20},{16,8},{20,12},{24,0},{28,4},{1,25},{... | collective-permute-start | bytes 786440 | tf_op jit(solution)/shard_map/ppermute | solution.py:17
  160.8 26.5 %collective-permute-start.33 = (f32[128,256]{1,0:T(8,128)S(1)}, f32[128,256]{1,0:T(8,128)S(1)}, u32[]{:S(2)}, u32[]{:S(2)}) collective-permute-start(f32[128,256]{1,0:T(8,128)S(1)} %slice_select_fusion.4), channel_id=1, source_target_pairs={{0,2},{1,3},{2,0},{3,1},{4,6},{5,7},{6,4},{7,5},{8,10},{9,11},{10,... | collective-permute-start | bytes 393224 | tf_op jit(solution)/shard_map/ppermute | solution.py:17
  183.4 15.9 %collective-permute-start.29 = (f16[512,256]{1,0:T(8,128)(2,1)S(1)}, f16[512,256]{1,0:T(8,128)(2,1)S(1)}, u32[]{:S(2)}, u32[]{:S(2)}) collective-permute-start(f16[512,256]{1,0:T(8,128)(2,1)S(1)} %broadcast_add_fusion), channel_id=1, source_target_pairs={{0,4},{4,0},{8,12},{12,8},{16,20},{20,16},{24,28},{28,24},{1,5},{5... | collective-permute-start | bytes 786440 | tf_op jit(solution)/shard_map/ppermute | solution.py:17
  185.7 12.6 %collective-permute-start.25 = (f16[512,256]{1,0:T(8,128)(2,1)S(1)}, f16[512,256]{1,0:T(8,128)(2,1)S(1)}, u32[]{:S(2)}, u32[]{:S(2)}) collective-permute-start(f16[512,256]{1,0:T(8,128)(2,1)S(1)} %collective-permute-done.24), channel_id=1, source_target_pairs={{0,4},{4,0},{8,12},{12,8},{16,20},{20,16},{24,28},{28,24},{1,5},{5... | collective-permute-start | bytes 786440 | tf_op jit(solution)/shard_map/ppermute | solution.py:17
  188.0 29.3 %collective-permute-start.34 = (f32[128,256]{1,0:T(8,128)}, f32[128,256]{1,0:T(8,128)}, u32[]{:S(2)}, u32[]{:S(2)}) collective-permute-start(f32[128,256]{1,0:T(8,128)} %get-tuple-element.38), channel_id=1, source_target_pairs={{0,4},{4,0},{8,12},{12,8},{16,20},{20,16},{24,28},{28,24},{1,5},{5... | collective-permute-start | bytes 393224 | tf_op jit(solution)/shard_map/ppermute | solution.py:17
  218.2 16.9 %collective-permute-start.35 = (f32[128,256]{1,0:T(8,128)S(1)}, f32[128,256]{1,0:T(8,128)S(1)}, u32[]{:S(2)}, u32[]{:S(2)}) collective-permute-start(f32[128,256]{1,0:T(8,128)S(1)} %get-tuple-element.36), channel_id=1, source_target_pairs={{0,8},{4,12},{8,0},{12,4},{16,24},{20,28},{24,16},{28,20},{1,9},{5... | collective-permute-start | bytes 393224 | tf_op jit(solution)/shard_map/ppermute | solution.py:17
  218.4 9.3 %collective-permute-start.27 = (f16[512,256]{1,0:T(8,128)(2,1)S(1)}, f16[512,256]{1,0:T(8,128)(2,1)S(1)}, u32[]{:S(2)}, u32[]{:S(2)}) collective-permute-start(f16[512,256]{1,0:T(8,128)(2,1)S(1)} %broadcast_add_fusion.1), channel_id=1, source_target_pairs={{0,4},{4,0},{8,12},{12,8},{16,20},{20,16},{24,28},{28,24},{1,5},{5... | collective-permute-start | bytes 786440 | tf_op jit(solution)/shard_map/ppermute | solution.py:17
  235.1 18.5 %collective-permute-start.30 = (f32[2,512,256]{2,1,0:T(8,128)S(1)}, f32[2,512,256]{2,1,0:T(8,128)S(1)}, u32[]{:S(2)}, u32[]{:S(2)}) collective-permute-start(f32[2,512,256]{2,1,0:T(8,128)S(1)} %select_bitcast_fusion), channel_id=1, source_target_pairs={{0,1},{1,0},{2,3},{3,2},{4,5},{5,4},{6,7},{7,6},{8,9},{9,8},{10,11... | collective-permute-start | bytes 3145736 | tf_op jit(solution)/shard_map/ppermute | solution.py:17
  235.2 9.7 %collective-permute-start.36 = (f32[128,256]{1,0:T(8,128)S(1)}, f32[128,256]{1,0:T(8,128)S(1)}, u32[]{:S(2)}, u32[]{:S(2)}) collective-permute-start(f32[128,256]{1,0:T(8,128)S(1)} %get-tuple-element.34), channel_id=1, source_target_pairs={{0,16},{4,20},{8,24},{12,28},{16,0},{20,4},{24,8},{28,12},{1,17},{... | collective-permute-start | bytes 393224 | tf_op jit(solution)/shard_map/ppermute | solution.py:17
  244.9 8.6 %collective-permute-start.37 = (f32[128,256]{1,0:T(8,128)S(1)}, f32[128,256]{1,0:T(8,128)S(1)}, u32[]{:S(2)}, u32[]{:S(2)}) collective-permute-start(f32[128,256]{1,0:T(8,128)S(1)} %add_add_fusion), channel_id=1, source_target_pairs={{0,2},{1,3},{2,0},{3,1},{4,6},{5,7},{6,4},{7,5},{8,10},{9,11},{10,... | collective-permute-start | bytes 393224 | tf_op jit(solution)/shard_map/ppermute | solution.py:17
  253.5 8.0 %collective-permute-start.38 = (f32[256,256]{1,0:T(8,128)S(1)}, f32[256,256]{1,0:T(8,128)S(1)}, u32[]{:S(2)}, u32[]{:S(2)}) collective-permute-start(f32[256,256]{1,0:T(8,128)S(1)} %pad_maximum_fusion.5), channel_id=1, source_target_pairs={{0,1},{1,0},{2,3},{3,2},{4,5},{5,4},{6,7},{7,6},{8,9},{9,8},{10,11... | collective-permute-start | bytes 786440 | tf_op jit(solution)/shard_map/ppermute | solution.py:17
  260.8 8.9 %collective-permute-start.31 = (f16[1,528,256]{2,1,0:T(8,128)(2,1)S(1)}, f16[1,528,256]{2,1,0:T(8,128)(2,1)S(1)}, u32[]{:S(2)}, u32[]{:S(2)}) collective-permute-start(f16[1,528,256]{2,1,0:T(8,128)(2,1)S(1)} %concatenate.46), channel_id=1, source_target_pairs={{0,2},{1,3},{2,0},{3,1},{4,6},{5,7},{6,4},{7,5},{8,10},{9,11},{10,... | collective-permute-start | bytes 811016 | tf_op jit(solution)/shard_map/ppermute | solution.py:17
  272.5 1.4 collective-permute-start.39
  274.0 4.3 %collective-permute-start.40 = (f32[64,256]{1,0:T(8,128)S(1)}, f32[64,256]{1,0:T(8,128)S(1)}, u32[]{:S(2)}, u32[]{:S(2)}) collective-permute-start(f32[64,256]{1,0:T(8,128)S(1)} %slice_select_fusion.6), channel_id=1, source_target_pairs={{0,2},{1,3},{2,0},{3,1},{4,6},{5,7},{6,4},{7,5},{8,10},{9,11},{10,... | collective-permute-start | bytes 196616 | tf_op jit(solution)/shard_map/ppermute | solution.py:17
  278.3 7.8 %collective-permute-start.41 = (f32[64,256]{1,0:T(8,128)S(1)}, f32[64,256]{1,0:T(8,128)S(1)}, u32[]{:S(2)}, u32[]{:S(2)}) collective-permute-start(f32[64,256]{1,0:T(8,128)S(1)} %select_add_fusion.5), channel_id=1, source_target_pairs={{0,4},{4,0},{8,12},{12,8},{16,20},{20,16},{24,28},{28,24},{1,5},{5... | collective-permute-start | bytes 196616 | tf_op jit(solution)/shard_map/ppermute | solution.py:17
  286.1 7.7 %collective-permute-start.42 = (f32[64,256]{1,0:T(8,128)S(1)}, f32[64,256]{1,0:T(8,128)S(1)}, u32[]{:S(2)}, u32[]{:S(2)}) collective-permute-start(f32[64,256]{1,0:T(8,128)S(1)} %add_add_fusion.2), channel_id=1, source_target_pairs={{0,8},{4,12},{8,0},{12,4},{16,24},{20,28},{24,16},{28,20},{1,9},{5... | collective-permute-start | bytes 196616 | tf_op jit(solution)/shard_map/ppermute | solution.py:17
  293.8 5.2 %collective-permute-start.43 = (f32[64,256]{1,0:T(8,128)S(1)}, f32[64,256]{1,0:T(8,128)S(1)}, u32[]{:S(2)}, u32[]{:S(2)}) collective-permute-start(f32[64,256]{1,0:T(8,128)S(1)} %add_add_fusion.1), channel_id=1, source_target_pairs={{0,16},{4,20},{8,24},{12,28},{16,0},{20,4},{24,8},{28,12},{1,17},{... | collective-permute-start | bytes 196616 | tf_op jit(solution)/shard_map/ppermute | solution.py:17
  299.1 4.3 %collective-permute-start.44 = (f32[64,256]{1,0:T(8,128)S(1)}, f32[64,256]{1,0:T(8,128)S(1)}, u32[]{:S(2)}, u32[]{:S(2)}) collective-permute-start(f32[64,256]{1,0:T(8,128)S(1)} %add.241), channel_id=1, source_target_pairs={{0,2},{1,3},{2,0},{3,1},{4,6},{5,7},{6,4},{7,5},{8,10},{9,11},{10,... | collective-permute-start | bytes 196616 | tf_op jit(solution)/shard_map/ppermute | solution.py:17
  303.5 1.4 collective-permute-start.45
  (20 other events, 101.7 us)
Sparse Core Ops, SparseCore 0:
  19.8 40.4 all-gather.2
  62.9 121.4 all-gather.4

commit v3 on v2

--- a/solution.py
+++ b/solution.py
@@ -460,7 +460,7 @@
     for mask, earlier in zip(bits_of("row"), partials):
         second_inner = second_inner + swap(after(second_inner, earlier), "row", mask)
 
-    signed_rows = negated(row_filtered, samples)
+    signed_rows = negated(after(row_filtered, partials[max(planes - 2, 0)]), samples)
     updated, written = None, []
     for part, waits in enumerate(([partial], [partial], [partial], [partial])):
         updated, row = update_part(
@@ -489,8 +489,8 @@
     gram = scatter_sum(inner(second, second))
     for i, mask in enumerate(bits_of("row")):
         gram = gram + swap(gram, "row", mask)
-        if i < 2:
-            gram = gram + written[2 + i]
+        if i in (0, 2):
+            gram = gram + written[2 + i // 2]
     basis = normalized(gather_parts(gram) / channels, second)
     return (updated, basis)
 

time: 337 us -> 350 us (1.039)
  starting transfers between devices: 78.7 us -> 94.3 us
  other arithmetic: 19.5 us -> 14.8 us
    ppermute x43, starting transfers between devices: 74.3 us -> 88.7 us  [swap(): lax.ppermute(cells, axis, [(i, i ^ mask) for i in range(lax.axis_size(axi...]
    unnamed x41 -> x43, local copies, waits for them, and re-layouts: 7.71 us -> 8.79 us
  transfers between devices with their start and end apart: 48 -> 48, of which waited for: 19 -> 22; matrix products, arithmetic and copies ran while one was open for 7% -> 6% of each run, Pallas kernels for 25% -> 24%
where the time goes in v3:
time: 350 us
  Pallas kernels  111 us (32%)
  starting transfers between devices  94.3 us (27%)
  waiting for transfers between devices  89.3 us (26%)
  between operations  22.6 us (6%)
  other arithmetic  14.8 us (4%)
  local copies, waits for them, and re-layouts  12.7 us (4%)
  matrix products  5.11 us (1%)
    ppermute x43, starting transfers between devices, swap(): lax.ppermute(cells, axis, [(i, i ^ mask) for i in range(lax.axis_size(axi...  88.7 us
    ppermute x43, waiting for transfers between devices, swap(): lax.ppermute(cells, axis, [(i, i ^ mask) for i in range(lax.axis_size(axi...  85.3 us
    pallas_call x4, Pallas kernels, update_part(): pl.pallas_call(functools.partial(update_kernel, scale), grid=(steps,), in...  28.1 us
    pallas_call x4, Pallas kernels, second_part(): pl.pallas_call(functools.partial(second_kernel, before is not None), grid...  27.8 us
    pallas_call x4, Pallas kernels, first_part(): pl.pallas_call(functools.partial(first_kernel, blocks), grid_spec=pltpu.P...  26.7 us
    pallas_call x1, Pallas kernels, normalized(): pl.pallas_call(functools.partial(basis_kernel, min(count, 64)), out_shape...  24.6 us
    unnamed x43, local copies, waits for them, and re-layouts  8.79 us
  transfers between devices with their start and end apart: 48, of which 22 were waited for; matrix products, arithmetic and copies ran while one was open for 6% of the time, Pallas kernels for 24%

profile of v3, /device:TPU:0, one launch (start us, length us, event | category | flops | bytes accessed | tf_op | source)
XLA Modules:
  0.0 349.6 jit_solution(3360253378140964696)
XLA Ops:
  8.0 2.4 collective-permute-start
  11.7 3.9 %collective-permute-done.1.below = f32[4,512]{1,0:T(4,128)S(1)} collective-permute-done((f32[4,512]{1,0:T(4,128)S(1)}, f32[4,512]{1,0:T(4,128)S(1)}, u32[]{:S(2)}, u32[]{:S(2)}) %collective-permute-start.1) | collective-permute-done | bytes 8224 | tf_op jit(solution)/shard_map/ppermute | solution.py:315
  16.2 3.4 filter_stripe.1
  19.6 1.8 collective-permute-start.7
  22.7 31.1 %collective-permute-start.5 = (bf16[512,512]{1,0:T(8,128)(2,1)S(1)}, bf16[512,512]{1,0:T(8,128)(2,1)S(1)}, u32[]{:S(2)}, u32[]{:S(2)}) collective-permute-start(bf16[512,512]{1,0:T(8,128)(2,1)S(1)} %pad_maximum_fusion.1.refs_1_), channel_id=1, source_target_pairs={{0,2},{1,3},{2,0},{3,1},{4,6},{5,7},{6,4},{7,5},{8,10},{9,11},{10,... | collective-permute-start | bytes 1572872 | tf_op jit(solution)/shard_map/ppermute | solution.py:17
  54.6 8.6 %collective-permute-start.2 = (f32[256,256]{1,0:T(8,128)S(1)}, f32[256,256]{1,0:T(8,128)S(1)}, u32[]{:S(2)}, u32[]{:S(2)}) collective-permute-start(f32[256,256]{1,0:T(8,128)S(1)} %slice_select_fusion.2), channel_id=1, source_target_pairs={{0,1},{1,0},{2,3},{3,2},{4,5},{5,4},{6,7},{7,6},{8,9},{9,8},{10,11... | collective-permute-start | bytes 786440 | tf_op jit(solution)/shard_map/ppermute | solution.py:17
  64.6 4.2 %collective-permute-start.10 = (f32[8,128]{1,0:T(8,128)S(1)}, f32[8,128]{1,0:T(8,128)S(1)}, u32[]{:S(2)}, u32[]{:S(2)}) collective-permute-start(f32[8,128]{1,0:T(8,128)S(1)} %broadcast_in_dim.4), channel_id=1, source_target_pairs={{0,24},{4,28},{8,16},{12,20},{16,8},{20,12},{24,0},{28,4},{1,25},{... | collective-permute-start | bytes 12296 | tf_op jit(solution)/shard_map/ppermute | solution.py:17
  74.1 1.8 collective-permute-start.11
  75.9 1.9 collective-permute-done.11
  79.3 3.3 collective-permute-done.13
  85.1 6.7 %first_part.7 = (f32[256,640]{1,0:T(8,128)S(1)}, f32[256,640]{1,0:T(8,128)S(1)}) custom-call(s32[6]{0:T(128)S(1)} %stack.96.place, f32[256,128]{1,0:T(8,128)S(1)} %turned.2.refs_0_, bf16[512,512]{1,0:T(8,128)(2,1)S(1)} %pad_maximum_fusion.1.refs_1_, bf16[512,512]{1,0:T(8,128)(2,1)S(1)} %collective-permute-done.4.refs_2_, ...), custom_call_target="tpu_custom_call" | custom-call | flops 3221225472 | bytes 8388608 | tf_op jit(solution)/shard_map/first_part/pallas_call | solution.py:138
  91.9 1.7 collective-permute-start.19
  93.6 6.9 %first_part.4 = (f32[256,640]{1,0:T(8,128)S(1)}, f32[256,640]{1,0:T(8,128)S(1)}) custom-call(s32[6]{0:T(128)S(1)} %stack.92.place, f32[256,128]{1,0:T(8,128)S(1)} %turned.2.refs_0_, bf16[512,512]{1,0:T(8,128)(2,1)S(1)} %pad_maximum_fusion.1.refs_1_, bf16[512,512]{1,0:T(8,128)(2,1)S(1)} %collective-permute-done.4.refs_2_, ...), custom_call_target="tpu_custom_call" | custom-call | flops 3221225472 | bytes 8388608 | tf_op jit(solution)/shard_map/first_part/pallas_call | solution.py:138
  100.6 6.5 %first_part.6 = (f32[256,640]{1,0:T(8,128)S(1)}, f32[256,640]{1,0:T(8,128)S(1)}) custom-call(s32[6]{0:T(128)S(1)} %stack.93.place, f32[256,128]{1,0:T(8,128)S(1)} %turned.2.refs_0_, bf16[512,512]{1,0:T(8,128)(2,1)S(1)} %pad_maximum_fusion.1.refs_1_, bf16[512,512]{1,0:T(8,128)(2,1)S(1)} %collective-permute-done.4.refs_2_, ...), custom_call_target="tpu_custom_call" | custom-call | flops 3221225472 | bytes 8388608 | tf_op jit(solution)/shard_map/first_part/pallas_call | solution.py:138
  107.2 2.1 collective-permute-start.17
  109.3 12.5 %collective-permute-done.14 = f16[256,640]{1,0:T(8,128)(2,1)S(1)} collective-permute-done((f16[256,640]{1,0:T(8,128)(2,1)S(1)}, f16[256,640]{1,0:T(8,128)(2,1)S(1)}, u32[]{:S(2)}, u32[]{:S(2)}) %collective-permute-start.14) | collective-permute-done | bytes 327712 | tf_op jit(solution)/shard_map/ppermute | solution.py:17
  122.3 6.3 %collective-permute-start.20 = (f16[256,640]{1,0:T(8,128)(2,1)S(1)}, f16[256,640]{1,0:T(8,128)(2,1)S(1)}, u32[]{:S(2)}, u32[]{:S(2)}) collective-permute-start(f16[256,640]{1,0:T(8,128)(2,1)S(1)} %add_convert_fusion), channel_id=1, source_target_pairs={{0,8},{4,12},{8,0},{12,4},{16,24},{20,28},{24,16},{28,20},{1,9},{5... | collective-permute-start | bytes 983048 | tf_op jit(solution)/shard_map/ppermute | solution.py:17
  128.6 5.7 %collective-permute-done.17 = f16[256,640]{1,0:T(8,128)(2,1)S(1)} collective-permute-done((f16[256,640]{1,0:T(8,128)(2,1)S(1)}, f16[256,640]{1,0:T(8,128)(2,1)S(1)}, u32[]{:S(2)}, u32[]{:S(2)}) %collective-permute-start.17) | collective-permute-done | bytes 327712 | tf_op jit(solution)/shard_map/ppermute | solution.py:17
  134.3 6.2 %collective-permute-start.18 = (f16[256,640]{1,0:T(8,128)(2,1)S(1)}, f16[256,640]{1,0:T(8,128)(2,1)S(1)}, u32[]{:S(2)}, u32[]{:S(2)}) collective-permute-start(f16[256,640]{1,0:T(8,128)(2,1)S(1)} %add_convert_fusion.1), channel_id=1, source_target_pairs={{0,16},{4,20},{8,24},{12,28},{16,0},{20,4},{24,8},{28,12},{1,17},{... | collective-permute-start | bytes 983048 | tf_op jit(solution)/shard_map/ppermute | solution.py:17
  140.6 6.5 %first_part.5 = (f32[256,640]{1,0:T(8,128)S(1)}, f32[256,640]{1,0:T(8,128)S(1)}) custom-call(s32[6]{0:T(128)S(1)} %stack.89.place, f32[256,128]{1,0:T(8,128)S(1)} %turned.2.refs_0_, bf16[512,512]{1,0:T(8,128)(2,1)S(1)} %pad_maximum_fusion.1.refs_1_, bf16[512,512]{1,0:T(8,128)(2,1)S(1)} %collective-permute-done.4.refs_2_, ...), custom_call_target="tpu_custom_call" | custom-call | flops 3221225472 | bytes 8388608 | tf_op jit(solution)/shard_map/first_part/pallas_call | solution.py:138
  147.3 2.5 collective-permute-start.16
  149.9 15.8 %collective-permute-done.18 = f16[256,640]{1,0:T(8,128)(2,1)S(1)} collective-permute-done((f16[256,640]{1,0:T(8,128)(2,1)S(1)}, f16[256,640]{1,0:T(8,128)(2,1)S(1)}, u32[]{:S(2)}, u32[]{:S(2)}) %collective-permute-start.18) | collective-permute-done | bytes 327712 | tf_op jit(solution)/shard_map/ppermute | solution.py:17
  166.7 4.5 %collective-permute-done.21 = f32[128,256]{1,0:T(8,128)S(1)} collective-permute-done((f32[128,256]{1,0:T(8,128)S(1)}, f32[128,256]{1,0:T(8,128)S(1)}, u32[]{:S(2)}, u32[]{:S(2)}) %collective-permute-start.21) | collective-permute-done | bytes 131104 | tf_op jit(solution)/shard_map/ppermute | solution.py:17
  173.6 1.8 collective-permute-start.23
  175.4 2.0 collective-permute-start.24
  177.8 2.3 collective-permute-start.28
  181.0 2.7 collective-permute-done.24
  183.8 6.8 %second_part.4.refs_6_ = f32[2048,256]{1,0:T(8,128)S(1)} custom-call(s32[2]{0:T(128)S(1)} %pad_add_fusion.1.place, f32[2048,4096]{1,0:T(8,128)} %tile.7, f32[2048,4096]{1,0:T(8,128)} %tile.7, bf16[512,256]{1,0:T(8,128)(2,1)S(1)} %get-tuple-element.49.refs_2_, bf16[512,256]{1,0:T(8,128)(2,1)S(1)} %get-tuple-element.48.refs_3_, ...), custom_call_target="tpu_custom_call" | custom-call | flops 3221225472 | bytes 8388608 | tf_op jit(solution)/shard_map/second_part/pallas_call | solution.py:229
  192.3 1.8 collective-permute-start.25
  194.2 2.1 collective-permute-start.33
  202.6 4.4 %collective-permute-done.27 = f16[512,256]{1,0:T(8,128)(2,1)S(1)} collective-permute-done((f16[512,256]{1,0:T(8,128)(2,1)S(1)}, f16[512,256]{1,0:T(8,128)(2,1)S(1)}, u32[]{:S(2)}, u32[]{:S(2)}) %collective-permute-start.27) | collective-permute-done | bytes 262176 | tf_op jit(solution)/shard_map/ppermute | solution.py:17
  208.0 2.2 copy-done
  213.0 7.1 %second_part.5.refs_6_ = f32[2048,256]{1,0:T(8,128)S(1)} custom-call(s32[2]{0:T(128)S(1)} %pad_add_fusion.2.place, f32[2048,4096]{1,0:T(8,128)} %tile.7, f32[2048,4096]{1,0:T(8,128)} %tile.7, bf16[512,256]{1,0:T(8,128)(2,1)S(1)} %copy-done.9, bf16[512,256]{1,0:T(8,128)(2,1)S(1)} %get-tuple-element.71.refs_3_, bf16[512,256]{1,0:T(8,128)(2,1)S(1)} %copy-done.13, ...), custom_call_target="tpu_custom_call" | custom-call | flops 3221225472 | bytes 8388608 | tf_op jit(solution)/shard_map/second_part/pallas_call | solution.py:229
  220.6 6.8 %second_part.6.refs_6_ = f32[2048,256]{1,0:T(8,128)S(1)} custom-call(s32[2]{0:T(128)S(1)} %pad_add_fusion.place, f32[2048,4096]{1,0:T(8,128)} %tile.7, f32[2048,4096]{1,0:T(8,128)} %tile.7, bf16[512,256]{1,0:T(8,128)(2,1)S(1)} %get-tuple-element.78.refs_2_, bf16[512,256]{1,0:T(8,128)(2,1)S(1)} %get-tuple-element.77.refs_3_, bf16[512,256]{1,0:T(8,128)(2,1)S(1)} %copy-done.11, ...), custom_call_target="tpu_custom_call" | custom-call | flops 3221225472 | bytes 8388608 | tf_op jit(solution)/shard_map/second_part/pallas_call | solution.py:229
  231.9 1.7 broadcast_add_fusion
  238.2 2.8 collective-permute-done.29
  241.2 7.1 %second_part.7.rest_0_.rest_1_ = f32[2048,256]{1,0:T(8,128)S(1)} custom-call(s32[2]{0:T(128)S(1)} %pad_add_fusion.3.place, f32[2048,4096]{1,0:T(8,128)} %tile.7, f32[2048,4096]{1,0:T(8,128)} %tile.7, bf16[512,256]{1,0:T(8,128)(2,1)S(1)} %get-tuple-element.68.refs_2_, bf16[512,256]{1,0:T(8,128)(2,1)S(1)} %get-tuple-element.67.refs_3_, ...), custom_call_target="tpu_custom_call" | custom-call | flops 3221225472 | bytes 8388608 | tf_op jit(solution)/shard_map/second_part/pallas_call | solution.py:229
  250.1 6.9 %update_part.4 = (f32[2048,4096]{1,0:T(8,128)}, f32[1,256]{1,0:T(1,128)S(1)}) custom-call(f32[2048,4096]{1,0:T(8,128)} %tile.7, bf16[2048,512]{1,0:T(8,128)(2,1)S(1)} %pad_maximum_fusion.rows, bf16[4096,512]{1,0:T(8,128)(2,1)S(1)} %copy-done.1, f32[2048,256]{1,0:T(8,128)S(1)} %second_part.7.rest_0_.rest_1_), custom_call_target="tpu_custom_call" | custom-call | flops 2147483648 | bytes 16777216 | tf_op jit(solution)/shard_map/update_part/pallas_call | solution.py:267
  258.2 1.8 collective-permute-start.37
  260.1 6.9 %update_part.5 = (f32[2048,4096]{1,0:T(8,128)}, f32[1,256]{1,0:T(1,128)S(1)}) custom-call(f32[2048,4096]{1,0:T(8,128)} %tile.7, bf16[2048,512]{1,0:T(8,128)(2,1)S(1)} %pad_maximum_fusion.rows, bf16[4096,512]{1,0:T(8,128)(2,1)S(1)} %copy-done.1, f32[2048,4096]{1,0:T(8,128)} %get-tuple-element.26.rest_0_, ...), custom_call_target="tpu_custom_call", output_to_operand_aliasing={{0}: (3, {})} | custom-call | flops 2147483648 | bytes 16777216 | tf_op jit(solution)/shard_map/update_part/pallas_call | solution.py:267
  268.4 1.9 abs_reduce_fusion
  274.8 8.2 %collective-permute-done.31 = f16[1,528,256]{2,1,0:T(8,128)(2,1)S(1)} collective-permute-done((f16[1,528,256]{2,1,0:T(8,128)(2,1)S(1)}, f16[1,528,256]{2,1,0:T(8,128)(2,1)S(1)}, u32[]{:S(2)}, u32[]{:S(2)}) %collective-permute-start.31) | collective-permute-done | bytes 270368 | tf_op jit(solution)/shard_map/ppermute | solution.py:17
  287.6 4.0 %collective-permute-done.40 = f32[64,256]{1,0:T(8,128)S(1)} collective-permute-done((f32[64,256]{1,0:T(8,128)S(1)}, f32[64,256]{1,0:T(8,128)S(1)}, u32[]{:S(2)}, u32[]{:S(2)}) %collective-permute-start.40) | collective-permute-done | bytes 65568 | tf_op jit(solution)/shard_map/ppermute | solution.py:17
  292.3 7.1 %update_part.6 = (f32[2048,4096]{1,0:T(8,128)}, f32[1,256]{1,0:T(1,128)S(1)}) custom-call(f32[2048,4096]{1,0:T(8,128)} %tile.7, bf16[2048,512]{1,0:T(8,128)(2,1)S(1)} %copy-done.4, bf16[4096,512]{1,0:T(8,128)(2,1)S(1)} %copy-done.2, f32[2048,4096]{1,0:T(8,128)} %get-tuple-element.27.rest_0_, ...), custom_call_target="tpu_custom_call", output_to_operand_aliasing={{0}: (3, {})} | custom-call | flops 2147483648 | bytes 16777216 | tf_op jit(solution)/shard_map/update_part/pallas_call | solution.py:267
  299.5 4.3 %collective-permute-done.42 = f32[64,256]{1,0:T(8,128)S(1)} collective-permute-done((f32[64,256]{1,0:T(8,128)S(1)}, f32[64,256]{1,0:T(8,128)S(1)}, u32[]{:S(2)}, u32[]{:S(2)}) %collective-permute-start.42) | collective-permute-done | bytes 65568 | tf_op jit(solution)/shard_map/ppermute | solution.py:17
  305.2 7.1 %update_part.7 = (f32[2048,4096]{1,0:T(8,128)}, f32[1,256]{1,0:T(1,128)S(1)}) custom-call(f32[2048,4096]{1,0:T(8,128)} %tile.7, bf16[2048,512]{1,0:T(8,128)(2,1)S(1)} %copy-done.4, bf16[4096,512]{1,0:T(8,128)(2,1)S(1)} %copy-done.2, f32[2048,4096]{1,0:T(8,128)} %get-tuple-element.28.rest_0_, ...), custom_call_target="tpu_custom_call", output_to_operand_aliasing={{0}: (3, {})} | custom-call | flops 2147483648 | bytes 16777216 | tf_op jit(solution)/shard_map/update_part/pallas_call | solution.py:267
  312.7 4.0 %collective-permute-done.44 = f32[64,256]{1,0:T(8,128)S(1)} collective-permute-done((f32[64,256]{1,0:T(8,128)S(1)}, f32[64,256]{1,0:T(8,128)S(1)}, u32[]{:S(2)}, u32[]{:S(2)}) %collective-permute-start.44) | collective-permute-done | bytes 65568 | tf_op jit(solution)/shard_map/ppermute | solution.py:17
  318.2 24.6 %normalized.1 = f32[512,256]{1,0:T(8,128)} custom-call(f32[256,256]{1,0:T(8,128)S(1)} %maximum_multiply_fusion.gram, f32[512,256]{1,0:T(8,128)S(1)} %fusion.15.vectors), custom_call_target="tpu_custom_call" | custom-call | tf_op jit(solution)/shard_map/normalized/pallas_call | solution.py:377
  (198 shorter events, 51.9 us)
Async XLA Ops:
  7.2 200.8 %all-gather.5.cloned.1.call-start = ((), (), s32[]{:S(2)}) async-start(), calls=%async_computation.1 | async-start | bytes 4718592 | tf_op jit(solution)/shard_map/all_gather | solution.py:425
  8.0 3.7 %collective-permute-start = (f32[4,512]{1,0:T(4,128)S(1)}, f32[4,512]{1,0:T(4,128)S(1)}, u32[]{:S(2)}, u32[]{:S(2)}) collective-permute-start(f32[4,512]{1,0:T(4,128)S(1)} %pad_maximum_fusion.7), channel_id=1, source_target_pairs={{0,1},{1,2},{2,3},{3,4},{4,5},{5,6},{6,7},{7,8},{8,9},{9,10},{10,1... | collective-permute-start | bytes 24584 | tf_op jit(solution)/shard_map/ppermute | solution.py:314
  10.4 5.2 %collective-permute-start.1 = (f32[4,512]{1,0:T(4,128)S(1)}, f32[4,512]{1,0:T(4,128)S(1)}, u32[]{:S(2)}, u32[]{:S(2)}) collective-permute-start(f32[4,512]{1,0:T(4,128)S(1)} %pad_maximum_fusion.8), channel_id=1, source_target_pairs={{1,0},{2,1},{3,2},{4,3},{5,4},{6,5},{7,6},{8,7},{9,8},{10,9},{11,1... | collective-permute-start | bytes 24584 | tf_op jit(solution)/shard_map/ppermute | solution.py:315
  19.6 1.8 collective-permute-start.7
  22.3 209.6 %all-gather.3.cloned.1.call-start = ((), (), s32[]{:S(2)}) async-start(), calls=%async_computation | async-start | bytes 2621440 | tf_op jit(solution)/shard_map/all_gather | solution.py:424
  22.7 46.9 %collective-permute-start.5 = (bf16[512,512]{1,0:T(8,128)(2,1)S(1)}, bf16[512,512]{1,0:T(8,128)(2,1)S(1)}, u32[]{:S(2)}, u32[]{:S(2)}) collective-permute-start(bf16[512,512]{1,0:T(8,128)(2,1)S(1)} %pad_maximum_fusion.1.refs_1_), channel_id=1, source_target_pairs={{0,2},{1,3},{2,0},{3,1},{4,6},{5,7},{6,4},{7,5},{8,10},{9,11},{10,... | collective-permute-start | bytes 1572872 | tf_op jit(solution)/shard_map/ppermute | solution.py:17
  54.6 14.3 %collective-permute-start.2 = (f32[256,256]{1,0:T(8,128)S(1)}, f32[256,256]{1,0:T(8,128)S(1)}, u32[]{:S(2)}, u32[]{:S(2)}) collective-permute-start(f32[256,256]{1,0:T(8,128)S(1)} %slice_select_fusion.2), channel_id=1, source_target_pairs={{0,1},{1,0},{2,3},{3,2},{4,5},{5,4},{6,7},{7,6},{8,9},{9,8},{10,11... | collective-permute-start | bytes 786440 | tf_op jit(solution)/shard_map/ppermute | solution.py:17
  63.2 21.8 %collective-permute-start.4 = (bf16[512,512]{1,0:T(8,128)(2,1)S(1)}, bf16[512,512]{1,0:T(8,128)(2,1)S(1)}, u32[]{:S(2)}, u32[]{:S(2)}) collective-permute-start(bf16[512,512]{1,0:T(8,128)(2,1)S(1)} %pad_maximum_fusion.1.refs_1_), channel_id=1, source_target_pairs={{0,1},{1,0},{2,3},{3,2},{4,5},{5,4},{6,7},{7,6},{8,9},{9,8},{10,11... | collective-permute-start | bytes 1572872 | tf_op jit(solution)/shard_map/ppermute | solution.py:17
  64.6 6.0 %collective-permute-start.10 = (f32[8,128]{1,0:T(8,128)S(1)}, f32[8,128]{1,0:T(8,128)S(1)}, u32[]{:S(2)}, u32[]{:S(2)}) collective-permute-start(f32[8,128]{1,0:T(8,128)S(1)} %broadcast_in_dim.4), channel_id=1, source_target_pairs={{0,24},{4,28},{8,16},{12,20},{16,8},{20,12},{24,0},{28,4},{1,25},{... | collective-permute-start | bytes 12296 | tf_op jit(solution)/shard_map/ppermute | solution.py:17
  68.8 4.6 %collective-permute-start.9 = (f32[8,128]{1,0:T(8,128)S(1)}, f32[8,128]{1,0:T(8,128)S(1)}, u32[]{:S(2)}, u32[]{:S(2)}) collective-permute-start(f32[8,128]{1,0:T(8,128)S(1)} %broadcast_in_dim.4), channel_id=1, source_target_pairs={{0,16},{4,20},{8,24},{12,28},{16,0},{20,4},{24,8},{28,12},{1,17},{... | collective-permute-start | bytes 12296 | tf_op jit(solution)/shard_map/ppermute | solution.py:17
  68.8 4.6 %collective-permute-start.8 = (f32[8,128]{1,0:T(8,128)S(1)}, f32[8,128]{1,0:T(8,128)S(1)}, u32[]{:S(2)}, u32[]{:S(2)}) collective-permute-start(f32[8,128]{1,0:T(8,128)S(1)} %broadcast_in_dim.4), channel_id=1, source_target_pairs={{0,8},{4,12},{8,0},{12,4},{16,24},{20,28},{24,16},{28,20},{1,9},{5... | collective-permute-start | bytes 12296 | tf_op jit(solution)/shard_map/ppermute | solution.py:17
  69.5 15.5 %collective-permute-start.6 = (bf16[512,512]{1,0:T(8,128)(2,1)S(1)}, bf16[512,512]{1,0:T(8,128)(2,1)S(1)}, u32[]{:S(2)}, u32[]{:S(2)}) collective-permute-start(bf16[512,512]{1,0:T(8,128)(2,1)S(1)} %collective-permute-done.5.refs_3_), channel_id=1, source_target_pairs={{0,1},{1,0},{2,3},{3,2},{4,5},{5,4},{6,7},{7,6},{8,9},{9,8},{10,11... | collective-permute-start | bytes 1572872 | tf_op jit(solution)/shard_map/ppermute | solution.py:17
  70.6 14.3 %collective-permute-start.3 = (f32[128,256]{1,0:T(8,128)S(1)}, f32[128,256]{1,0:T(8,128)S(1)}, u32[]{:S(2)}, u32[]{:S(2)}) collective-permute-start(f32[128,256]{1,0:T(8,128)S(1)} %slice_select_fusion.5), channel_id=1, source_target_pairs={{0,2},{1,3},{2,0},{3,1},{4,6},{5,7},{6,4},{7,5},{8,10},{9,11},{10,... | collective-permute-start | bytes 393224 | tf_op jit(solution)/shard_map/ppermute | solution.py:17
  74.1 3.7 %collective-permute-start.11 = (f32[8,128]{1,0:T(8,128)S(1)}, f32[8,128]{1,0:T(8,128)S(1)}, u32[]{:S(2)}, u32[]{:S(2)}) collective-permute-start(f32[8,128]{1,0:T(8,128)S(1)} %maximum_maximum_fusion), channel_id=1, source_target_pairs={{0,4},{4,0},{8,12},{12,8},{16,20},{20,16},{24,28},{28,24},{1,5},{5... | collective-permute-start | bytes 12296 | tf_op jit(solution)/shard_map/ppermute | solution.py:17
  77.8 1.2 collective-permute-start.12
  79.0 3.6 %collective-permute-start.13 = (f32[8,128]{1,0:T(8,128)S(1)}, f32[8,128]{1,0:T(8,128)S(1)}, u32[]{:S(2)}, u32[]{:S(2)}) collective-permute-start(f32[8,128]{1,0:T(8,128)S(1)} %max.29), channel_id=1, source_target_pairs={{0,2},{1,3},{2,0},{3,1},{4,6},{5,7},{6,4},{7,5},{8,10},{9,11},{10,... | collective-permute-start | bytes 12296 | tf_op jit(solution)/shard_map/ppermute | solution.py:17
  91.9 30.3 %collective-permute-start.19 = (f16[256,640]{1,0:T(8,128)(2,1)S(1)}, f16[256,640]{1,0:T(8,128)(2,1)S(1)}, u32[]{:S(2)}, u32[]{:S(2)}) collective-permute-start(f16[256,640]{1,0:T(8,128)(2,1)S(1)} %multiply_convert_fusion), channel_id=1, source_target_pairs={{0,4},{4,0},{8,12},{12,8},{16,20},{20,16},{24,28},{28,24},{1,5},{5... | collective-permute-start | bytes 983048 | tf_op jit(solution)/shard_map/ppermute | solution.py:17
  100.5 21.3 %collective-permute-start.14 = (f16[256,640]{1,0:T(8,128)(2,1)S(1)}, f16[256,640]{1,0:T(8,128)(2,1)S(1)}, u32[]{:S(2)}, u32[]{:S(2)}) collective-permute-start(f16[256,640]{1,0:T(8,128)(2,1)S(1)} %multiply_convert_fusion.3), channel_id=1, source_target_pairs={{0,4},{4,0},{8,12},{12,8},{16,20},{20,16},{24,28},{28,24},{1,5},{5... | collective-permute-start | bytes 983048 | tf_op jit(solution)/shard_map/ppermute | solution.py:17
  107.2 27.0 %collective-permute-start.17 = (f16[256,640]{1,0:T(8,128)(2,1)S(1)}, f16[256,640]{1,0:T(8,128)(2,1)S(1)}, u32[]{:S(2)}, u32[]{:S(2)}) collective-permute-start(f16[256,640]{1,0:T(8,128)(2,1)S(1)} %multiply_convert_fusion.1), channel_id=1, source_target_pairs={{0,4},{4,0},{8,12},{12,8},{16,20},{20,16},{24,28},{28,24},{1,5},{5... | collective-permute-start | bytes 983048 | tf_op jit(solution)/shard_map/ppermute | solution.py:17
  121.9 18.7 %collective-permute-start.15 = (f16[256,640]{1,0:T(8,128)(2,1)S(1)}, f16[256,640]{1,0:T(8,128)(2,1)S(1)}, u32[]{:S(2)}, u32[]{:S(2)}) collective-permute-start(f16[256,640]{1,0:T(8,128)(2,1)S(1)} %add_convert_fusion.2), channel_id=1, source_target_pairs={{0,24},{4,28},{8,16},{12,20},{16,8},{20,12},{24,0},{28,4},{1,25},{... | collective-permute-start | bytes 983048 | tf_op jit(solution)/shard_map/ppermute | solution.py:17
  122.3 27.6 %collective-permute-start.20 = (f16[256,640]{1,0:T(8,128)(2,1)S(1)}, f16[256,640]{1,0:T(8,128)(2,1)S(1)}, u32[]{:S(2)}, u32[]{:S(2)}) collective-permute-start(f16[256,640]{1,0:T(8,128)(2,1)S(1)} %add_convert_fusion), channel_id=1, source_target_pairs={{0,8},{4,12},{8,0},{12,4},{16,24},{20,28},{24,16},{28,20},{1,9},{5... | collective-permute-start | bytes 983048 | tf_op jit(solution)/shard_map/ppermute | solution.py:17
  134.3 31.3 %collective-permute-start.18 = (f16[256,640]{1,0:T(8,128)(2,1)S(1)}, f16[256,640]{1,0:T(8,128)(2,1)S(1)}, u32[]{:S(2)}, u32[]{:S(2)}) collective-permute-start(f16[256,640]{1,0:T(8,128)(2,1)S(1)} %add_convert_fusion.1), channel_id=1, source_target_pairs={{0,16},{4,20},{8,24},{12,28},{16,0},{20,4},{24,8},{28,12},{1,17},{... | collective-permute-start | bytes 983048 | tf_op jit(solution)/shard_map/ppermute | solution.py:17
  147.3 18.4 %collective-permute-start.16 = (f16[256,640]{1,0:T(8,128)(2,1)S(1)}, f16[256,640]{1,0:T(8,128)(2,1)S(1)}, u32[]{:S(2)}, u32[]{:S(2)}) collective-permute-start(f16[256,640]{1,0:T(8,128)(2,1)S(1)} %multiply_convert_fusion.2), channel_id=1, source_target_pairs={{0,4},{4,0},{8,12},{12,8},{16,20},{20,16},{24,28},{28,24},{1,5},{5... | collective-permute-start | bytes 983048 | tf_op jit(solution)/shard_map/ppermute | solution.py:17
  166.2 5.0 %collective-permute-start.21 = (f32[128,256]{1,0:T(8,128)S(1)}, f32[128,256]{1,0:T(8,128)S(1)}, u32[]{:S(2)}, u32[]{:S(2)}) collective-permute-start(f32[128,256]{1,0:T(8,128)S(1)} %slice_multiply_fusion.1), channel_id=1, source_target_pairs={{0,2},{1,3},{2,0},{3,1},{4,6},{5,7},{6,4},{7,5},{8,10},{9,11},{10,... | collective-permute-start | bytes 393224 | tf_op jit(solution)/shard_map/ppermute | solution.py:17
  171.3 1.6 collective-permute-start.22
  173.6 18.7 %collective-permute-start.23 = (f16[512,256]{1,0:T(8,128)(2,1)S(1)}, f16[512,256]{1,0:T(8,128)(2,1)S(1)}, u32[]{:S(2)}, u32[]{:S(2)}) collective-permute-start(f16[512,256]{1,0:T(8,128)(2,1)S(1)} %get-tuple-element.50), channel_id=1, source_target_pairs={{0,16},{4,20},{8,24},{12,28},{16,0},{20,4},{24,8},{28,12},{1,17},{... | collective-permute-start | bytes 786440 | tf_op jit(solution)/shard_map/ppermute | solution.py:17
  175.4 8.3 %collective-permute-start.24 = (f16[512,256]{1,0:T(8,128)(2,1)S(1)}, f16[512,256]{1,0:T(8,128)(2,1)S(1)}, u32[]{:S(2)}, u32[]{:S(2)}) collective-permute-start(f16[512,256]{1,0:T(8,128)(2,1)S(1)} %get-tuple-element.50), channel_id=1, source_target_pairs={{0,4},{4,0},{8,12},{12,8},{16,20},{20,16},{24,28},{28,24},{1,5},{5... | collective-permute-start | bytes 786440 | tf_op jit(solution)/shard_map/ppermute | solution.py:17
  177.4 19.0 %collective-permute-start.26 = (f16[512,256]{1,0:T(8,128)(2,1)S(1)}, f16[512,256]{1,0:T(8,128)(2,1)S(1)}, u32[]{:S(2)}, u32[]{:S(2)}) collective-permute-start(f16[512,256]{1,0:T(8,128)(2,1)S(1)} %get-tuple-element.50), channel_id=1, source_target_pairs={{0,8},{4,12},{8,0},{12,4},{16,24},{20,28},{24,16},{28,20},{1,9},{5... | collective-permute-start | bytes 786440 | tf_op jit(solution)/shard_map/ppermute | solution.py:17
  177.8 19.7 %collective-permute-start.28 = (f16[512,256]{1,0:T(8,128)(2,1)S(1)}, f16[512,256]{1,0:T(8,128)(2,1)S(1)}, u32[]{:S(2)}, u32[]{:S(2)}) collective-permute-start(f16[512,256]{1,0:T(8,128)(2,1)S(1)} %get-tuple-element.50), channel_id=1, source_target_pairs={{0,24},{4,28},{8,16},{12,20},{16,8},{20,12},{24,0},{28,4},{1,25},{... | collective-permute-start | bytes 786440 | tf_op jit(solution)/shard_map/ppermute | solution.py:17
  180.9 13.2 %collective-permute-start.32 = (f32[256,256]{1,0:T(8,128)S(1)}, f32[256,256]{1,0:T(8,128)S(1)}, u32[]{:S(2)}, u32[]{:S(2)}) collective-permute-start(f32[256,256]{1,0:T(8,128)S(1)} %slice_select_fusion.1), channel_id=1, source_target_pairs={{0,1},{1,0},{2,3},{3,2},{4,5},{5,4},{6,7},{7,6},{8,9},{9,8},{10,11... | collective-permute-start | bytes 786440 | tf_op jit(solution)/shard_map/ppermute | solution.py:17
  192.3 9.3 %collective-permute-start.25 = (f16[512,256]{1,0:T(8,128)(2,1)S(1)}, f16[512,256]{1,0:T(8,128)(2,1)S(1)}, u32[]{:S(2)}, u32[]{:S(2)}) collective-permute-start(f16[512,256]{1,0:T(8,128)(2,1)S(1)} %broadcast_add_fusion.2), channel_id=1, source_target_pairs={{0,4},{4,0},{8,12},{12,8},{16,20},{20,16},{24,28},{28,24},{1,5},{5... | collective-permute-start | bytes 786440 | tf_op jit(solution)/shard_map/ppermute | solution.py:17
  194.2 5.0 %collective-permute-start.33 = (f32[128,256]{1,0:T(8,128)S(1)}, f32[128,256]{1,0:T(8,128)S(1)}, u32[]{:S(2)}, u32[]{:S(2)}) collective-permute-start(f32[128,256]{1,0:T(8,128)S(1)} %slice_select_fusion.4), channel_id=1, source_target_pairs={{0,2},{1,3},{2,0},{3,1},{4,6},{5,7},{6,4},{7,5},{8,10},{9,11},{10,... | collective-permute-start | bytes 393224 | tf_op jit(solution)/shard_map/ppermute | solution.py:17
  196.4 10.6 %collective-permute-start.27 = (f16[512,256]{1,0:T(8,128)(2,1)S(1)}, f16[512,256]{1,0:T(8,128)(2,1)S(1)}, u32[]{:S(2)}, u32[]{:S(2)}) collective-permute-start(f16[512,256]{1,0:T(8,128)(2,1)S(1)} %collective-permute-done.26), channel_id=1, source_target_pairs={{0,4},{4,0},{8,12},{12,8},{16,20},{20,16},{24,28},{28,24},{1,5},{5... | collective-permute-start | bytes 786440 | tf_op jit(solution)/shard_map/ppermute | solution.py:17
  199.9 36.2 %collective-permute-start.34 = (f32[128,256]{1,0:T(8,128)}, f32[128,256]{1,0:T(8,128)}, u32[]{:S(2)}, u32[]{:S(2)}) collective-permute-start(f32[128,256]{1,0:T(8,128)} %get-tuple-element.38), channel_id=1, source_target_pairs={{0,4},{4,0},{8,12},{12,8},{16,20},{20,16},{24,28},{28,24},{1,5},{5... | collective-permute-start | bytes 393224 | tf_op jit(solution)/shard_map/ppermute | solution.py:17
  234.6 6.4 %collective-permute-start.29 = (f16[512,256]{1,0:T(8,128)(2,1)S(1)}, f16[512,256]{1,0:T(8,128)(2,1)S(1)}, u32[]{:S(2)}, u32[]{:S(2)}) collective-permute-start(f16[512,256]{1,0:T(8,128)(2,1)S(1)} %broadcast_add_fusion.1), channel_id=1, source_target_pairs={{0,4},{4,0},{8,12},{12,8},{16,20},{20,16},{24,28},{28,24},{1,5},{5... | collective-permute-start | bytes 786440 | tf_op jit(solution)/shard_map/ppermute | solution.py:17
  237.0 11.5 %collective-permute-start.35 = (f32[128,256]{1,0:T(8,128)S(1)}, f32[128,256]{1,0:T(8,128)S(1)}, u32[]{:S(2)}, u32[]{:S(2)}) collective-permute-start(f32[128,256]{1,0:T(8,128)S(1)} %get-tuple-element.36), channel_id=1, source_target_pairs={{0,8},{4,12},{8,0},{12,4},{16,24},{20,28},{24,16},{28,20},{1,9},{5... | collective-permute-start | bytes 393224 | tf_op jit(solution)/shard_map/ppermute | solution.py:17
  248.4 18.7 %collective-permute-start.30 = (f32[2,512,256]{2,1,0:T(8,128)S(1)}, f32[2,512,256]{2,1,0:T(8,128)S(1)}, u32[]{:S(2)}, u32[]{:S(2)}) collective-permute-start(f32[2,512,256]{2,1,0:T(8,128)S(1)} %select_bitcast_fusion), channel_id=1, source_target_pairs={{0,1},{1,0},{2,3},{3,2},{4,5},{5,4},{6,7},{7,6},{8,9},{9,8},{10,11... | collective-permute-start | bytes 3145736 | tf_op jit(solution)/shard_map/ppermute | solution.py:17
  248.6 9.7 %collective-permute-start.36 = (f32[128,256]{1,0:T(8,128)S(1)}, f32[128,256]{1,0:T(8,128)S(1)}, u32[]{:S(2)}, u32[]{:S(2)}) collective-permute-start(f32[128,256]{1,0:T(8,128)S(1)} %get-tuple-element.34), channel_id=1, source_target_pairs={{0,16},{4,20},{8,24},{12,28},{16,0},{20,4},{24,8},{28,12},{1,17},{... | collective-permute-start | bytes 393224 | tf_op jit(solution)/shard_map/ppermute | solution.py:17
  258.2 8.8 %collective-permute-start.37 = (f32[128,256]{1,0:T(8,128)S(1)}, f32[128,256]{1,0:T(8,128)S(1)}, u32[]{:S(2)}, u32[]{:S(2)}) collective-permute-start(f32[128,256]{1,0:T(8,128)S(1)} %add_add_fusion), channel_id=1, source_target_pairs={{0,2},{1,3},{2,0},{3,1},{4,6},{5,7},{6,4},{7,5},{8,10},{9,11},{10,... | collective-permute-start | bytes 393224 | tf_op jit(solution)/shard_map/ppermute | solution.py:17
  267.1 7.3 %collective-permute-start.38 = (f32[256,256]{1,0:T(8,128)S(1)}, f32[256,256]{1,0:T(8,128)S(1)}, u32[]{:S(2)}, u32[]{:S(2)}) collective-permute-start(f32[256,256]{1,0:T(8,128)S(1)} %pad_maximum_fusion.5), channel_id=1, source_target_pairs={{0,1},{1,0},{2,3},{3,2},{4,5},{5,4},{6,7},{7,6},{8,9},{9,8},{10,11... | collective-permute-start | bytes 786440 | tf_op jit(solution)/shard_map/ppermute | solution.py:17
  274.1 8.9 %collective-permute-start.31 = (f16[1,528,256]{2,1,0:T(8,128)(2,1)S(1)}, f16[1,528,256]{2,1,0:T(8,128)(2,1)S(1)}, u32[]{:S(2)}, u32[]{:S(2)}) collective-permute-start(f16[1,528,256]{2,1,0:T(8,128)(2,1)S(1)} %concatenate.46), channel_id=1, source_target_pairs={{0,2},{1,3},{2,0},{3,1},{4,6},{5,7},{6,4},{7,5},{8,10},{9,11},{10,... | collective-permute-start | bytes 811016 | tf_op jit(solution)/shard_map/ppermute | solution.py:17
  285.8 1.4 collective-permute-start.39
  287.3 4.3 %collective-permute-start.40 = (f32[64,256]{1,0:T(8,128)S(1)}, f32[64,256]{1,0:T(8,128)S(1)}, u32[]{:S(2)}, u32[]{:S(2)}) collective-permute-start(f32[64,256]{1,0:T(8,128)S(1)} %slice_select_fusion.6), channel_id=1, source_target_pairs={{0,2},{1,3},{2,0},{3,1},{4,6},{5,7},{6,4},{7,5},{8,10},{9,11},{10,... | collective-permute-start | bytes 196616 | tf_op jit(solution)/shard_map/ppermute | solution.py:17
  291.6 7.8 %collective-permute-start.41 = (f32[64,256]{1,0:T(8,128)S(1)}, f32[64,256]{1,0:T(8,128)S(1)}, u32[]{:S(2)}, u32[]{:S(2)}) collective-permute-start(f32[64,256]{1,0:T(8,128)S(1)} %select_add_fusion.5), channel_id=1, source_target_pairs={{0,4},{4,0},{8,12},{12,8},{16,20},{20,16},{24,28},{28,24},{1,5},{5... | collective-permute-start | bytes 196616 | tf_op jit(solution)/shard_map/ppermute | solution.py:17
  299.4 4.3 %collective-permute-start.42 = (f32[64,256]{1,0:T(8,128)S(1)}, f32[64,256]{1,0:T(8,128)S(1)}, u32[]{:S(2)}, u32[]{:S(2)}) collective-permute-start(f32[64,256]{1,0:T(8,128)S(1)} %add_add_fusion.2), channel_id=1, source_target_pairs={{0,8},{4,12},{8,0},{12,4},{16,24},{20,28},{24,16},{28,20},{1,9},{5... | collective-permute-start | bytes 196616 | tf_op jit(solution)/shard_map/ppermute | solution.py:17
  303.8 8.6 %collective-permute-start.43 = (f32[64,256]{1,0:T(8,128)S(1)}, f32[64,256]{1,0:T(8,128)S(1)}, u32[]{:S(2)}, u32[]{:S(2)}) collective-permute-start(f32[64,256]{1,0:T(8,128)S(1)} %add.245), channel_id=1, source_target_pairs={{0,16},{4,20},{8,24},{12,28},{16,0},{20,4},{24,8},{28,12},{1,17},{... | collective-permute-start | bytes 196616 | tf_op jit(solution)/shard_map/ppermute | solution.py:17
  312.3 4.3 %collective-permute-start.44 = (f32[64,256]{1,0:T(8,128)S(1)}, f32[64,256]{1,0:T(8,128)S(1)}, u32[]{:S(2)}, u32[]{:S(2)}) collective-permute-start(f32[64,256]{1,0:T(8,128)S(1)} %add_add_fusion.1), channel_id=1, source_target_pairs={{0,2},{1,3},{2,0},{3,1},{4,6},{5,7},{6,4},{7,5},{8,10},{9,11},{10,... | collective-permute-start | bytes 196616 | tf_op jit(solution)/shard_map/ppermute | solution.py:17
  316.7 1.4 collective-permute-start.45
  (21 other events, 146.3 us)
Sparse Core Ops, SparseCore 0:
  22.4 142.3 all-gather.4
  171.6 23.1 all-gather.2
